TPU v7x, 256 devices: a whole 4x4x8 slice. The times are simulated.
256 devices in a mesh: ctx: 64 (over x, z, core), head: 4 (over y).
Axes of the slice: x: 4, y: 4, z: 8, core: 2. Of those that a mesh axis runs over, the one named last changes fastest.
Arguments:
- queries: bfloat16 [8192, 16, 512], P('ctx', 'head'), may hold values from -5 to 5
- hist_keys: bfloat16 [131072, 16, 128], P('ctx', 'head'), may hold values from -5 to 5
- hist_values: bfloat16 [131072, 16, 128], P('ctx', 'head'), may hold values from -5 to 5
- own_keys: bfloat16 [8192, 16, 128], P('ctx', 'head'), may hold values from -5 to 5
- own_values: bfloat16 [8192, 16, 128], P('ctx', 'head'), may hold values from -5 to 5
- choices: int32 [16, 8192, 3], P('head', 'ctx'), may hold values from 0 to 63, all different within a row; in each aligned block of 128 rows (0 to 127, 128 to 255, ..., all dimensions but the last counted through in order) at most 8 rows name the same one
- positions: int32 [64, 128], P('ctx'), may hold values from 0 to 127, each once within a row
Outputs:
- attended: bfloat16 [8192, 16, 512], P(('ctx', 'head'))
Inputs may be any that keep to these rules, and one draw needn't show every extreme that they name: `choices`: the three numbers of a row differ; within the 128 tokens of one device in one group no block is chosen more than 8 times, and some block exactly 8 times. `positions`: each device's row holds each of 0 to 127 once.
All inputs are finite; a program needn't handle non-finite values.
Results may differ from a plain program's by a relative error of at most 0.0047.
Values may be sent and summed in bfloat16 or wider, within the bound.
No kernel may reach another device: no remote copies, remote signals or barrier semaphores. Data moves between devices by JAX's collectives and lax.ppermute only.
A program may use at most 128 MiB of HBM per device.

v0:
```python
import math

import jax
import jax.numpy as jnp
from jax import lax
from jax.sharding import PartitionSpec as P


def attend(query_rows, key_rows, value_rows, allowed, score_scale):
    scores = jnp.dot(query_rows, key_rows.T, preferred_element_type=jnp.float32) * score_scale
    if allowed is not None:
        scores = jnp.where(allowed, scores, -jnp.inf)
    highest = jnp.max(scores, axis=1, keepdims=True)
    weights = jnp.exp(scores - highest)
    denominator = jnp.sum(weights, axis=1, keepdims=True)
    blended = (
        jnp.dot(weights.astype(jnp.bfloat16), value_rows, preferred_element_type=jnp.float32)
        / denominator
    )
    return (blended, (highest + jnp.log(denominator))[:, 0])


def far_part(received, keys_moved, values_moved, score_scale):
    groups, sources, slot_depth, row_width = received.shape
    head_dim = keys_moved.shape[2]
    head_count = row_width // head_dim
    per_source = slot_depth * head_count
    row_limit = max(1, 2048 // per_source)
    step_size = math.gcd(sources, row_limit)

    def one_group(group_item):
        query_block, key_block, value_block = group_item
        row_blocks = query_block.reshape(sources // step_size, step_size * per_source, head_dim)

        def one_block(row_block):
            return attend(row_block, key_block, value_block, None, score_scale)

        blended, log_total = lax.map(one_block, row_blocks)
        return (
            blended.reshape(sources, slot_depth, row_width),
            log_total.reshape(sources, slot_depth, head_count),
        )

    return lax.map(one_group, (received, keys_moved, values_moved))


def local(queries, hist_keys, hist_values, own_keys, own_values, choices, positions):
    sources = lax.axis_size("ctx")
    row_count, groups, row_width = queries.shape
    head_dim = hist_keys.shape[2]
    head_count = row_width // head_dim
    capacity = 4 * row_count // sources
    score_scale = head_dim ** (-0.5)
    slot_count = sources * capacity
    block_ids = jnp.arange(sources, dtype=jnp.int32)
    one_hot = (choices[..., None] == block_ids).astype(jnp.int32)
    occupied = jnp.sum(one_hot, axis=2)
    earlier = jnp.cumsum(occupied, axis=1) - occupied
    slot_index = choices * capacity + jnp.sum(one_hot * earlier[:, :, None, :], axis=3)
    grouped = jnp.transpose(queries, (1, 0, 2))

    def fill_slots(group_rows, targets):
        empty_slots = jnp.zeros((slot_count, row_width), jnp.bfloat16)
        return empty_slots.at[targets.reshape(-1)].set(jnp.repeat(group_rows, 3, axis=0))

    outbound = jax.vmap(fill_slots)(grouped, slot_index)
    outbound = outbound.reshape(groups, sources, capacity, row_width)
    keys_moved = jnp.transpose(hist_keys, (1, 0, 2))
    values_moved = jnp.transpose(hist_values, (1, 0, 2))
    received = lax.all_to_all(outbound, "ctx", split_axis=1, concat_axis=1, tiled=True)
    far_out, far_lse = far_part(received, keys_moved, values_moved, score_scale)
    back_out, back_lse = (
        lax.all_to_all(far_out, "ctx", split_axis=1, concat_axis=1, tiled=True),
        lax.all_to_all(far_lse, "ctx", split_axis=1, concat_axis=1, tiled=True),
    )
    local_pos = positions[0]
    allowed = jnp.repeat(local_pos[None, :] <= local_pos[:, None], head_count, axis=0)

    def near_part(group_item):
        query_block, key_block, value_block = group_item
        blended, log_total = attend(
            query_block.reshape(row_count * head_count, head_dim),
            key_block,
            value_block,
            allowed,
            score_scale,
        )
        return (blended.reshape(row_count, row_width), log_total.reshape(row_count, head_count))

    own_out, own_lse = lax.map(
        near_part,
        (grouped, jnp.transpose(own_keys, (1, 0, 2)), jnp.transpose(own_values, (1, 0, 2))),
    )

    def take_rows(source_rows, indices):
        return source_rows[indices]

    flat_out = back_out.reshape(groups, slot_count, row_width)
    flat_lse = back_lse.reshape(groups, slot_count, head_count)
    got_out = jax.vmap(take_rows)(flat_out, slot_index)
    got_lse = jax.vmap(take_rows)(flat_lse, slot_index)
    all_lse = jnp.concatenate([own_lse[:, :, None, :], got_lse], axis=2)
    all_out = jnp.concatenate(
        [
            own_out.reshape(groups, row_count, 1, head_count, head_dim),
            got_out.reshape(groups, row_count, 3, head_count, head_dim),
        ],
        axis=2,
    )
    highest = jnp.max(all_lse, axis=2, keepdims=True)
    weights = jnp.exp(all_lse - highest)
    merged = jnp.sum(weights[..., None] * all_out, axis=2) / jnp.sum(weights, axis=2)[..., None]
    merged = jnp.transpose(
        merged.reshape(groups, row_count, row_width).astype(jnp.bfloat16), (1, 0, 2)
    )
    return lax.all_to_all(merged, "head", split_axis=0, concat_axis=1, tiled=True)


def solution(mesh):
    in_specs = (
        P("ctx", "head", None),
        P("ctx", "head", None),
        P("ctx", "head", None),
        P("ctx", "head", None),
        P("ctx", "head", None),
        P("head", "ctx", None),
        P("ctx", None),
    )
    out_specs = P(("ctx", "head"), None, None)
    return jax.shard_map(local, mesh=mesh, in_specs=in_specs, out_specs=out_specs, check_vma=False)
```

profile of v0, /device:TPU:1, one launch (start us, length us, event | category | flops | bytes accessed | tf_op | source)
XLA Modules:
  0.0 361.5 jit_solution(15523710859019317987)
XLA Ops:
  1.4 0.7 fusion.35
  2.5 0.7 multiply_reduce_fusion.1
  3.2 0.7 and_reduce_fusion
  4.0 1.1 copy.182
  5.7 2.5 reshape.192
  8.2 8.4 %scatter_custom_fusion = bf16[2048,512]{1,0:T(8,128)(2,1)S(1)} fusion(s32[1536]{0:T(1024)S(1)} %reshape.190, bf16[1536,512]{1,0:T(8,128)(2,1)} %reshape.192, bf16[]{:T(256)} %constant.53.clone.1), kind=kCustom, calls=%fused_computation.44 | custom fusion | bytes 2097664
  16.6 1.7 copy.141
  18.3 13.3 %all-to-all-start = ((bf16[4,64,8,512]{3,2,0,1:T(8,128)(2,1)}), bf16[4,64,8,512]{3,2,0,1:T(8,128)(2,1)}, u32[]{:S(2)}, u32[]{:S(2)}) async-start(bf16[4,64,8,512]{3,2,0,1:T(8,128)(2,1)} %copy.141), calls=%async_computation | async-start | bytes 4194304 | tf_op jit(solution)/shard_map/all_to_all | solution.py:70
  31.6 4.2 %copy_bitcast_fusion.1 = (bf16[4,2048,128]{2,1,0:T(8,128)(2,1)}, bf16[4,2048,128]{2,1,0:T(8,128)(2,1)}) fusion(bf16[2048,4,128]{2,1,0:T(4,128)(2,1)S(1)} %copy-done, bf16[2048,4,128]{2,1,0:T(4,128)(2,1)} %param.12), kind=kLoop, calls=%fused_computation.42 | loop fusion | bytes 8388608 | tf_op jit(solution)/shard_map/transpose | solution.py:69
  35.8 47.0 %all-to-all-done = bf16[4,64,8,512]{3,2,0,1:T(8,128)(2,1)} async-done(((bf16[4,64,8,512]{3,2,0,1:T(8,128)(2,1)}), bf16[4,64,8,512]{3,2,0,1:T(8,128)(2,1)}, u32[]{:S(2)}, u32[]{:S(2)}) %all-to-all-start) | async-done | bytes 2097184 | tf_op jit(solution)/shard_map/all_to_all | solution.py:70
  82.8 114.1 %while.30 = (s32[]{:T(128)}, f32[4,64,8,512]{3,2,0,1:T(8,128)}, f32[4,64,8,4]{2,3,0,1:T(4,128)S(1)}, bf16[4,64,8,512]{3,2,0,1:T(8,128)(2,1)}, bf16[4,2048,128]{2...) while((s32[]{:T(128)}, f32[4,64,8,512]{3,2,0,1:T(8,128)}, f32[4,64,8,4]{2,3,0,1:T(4,128)S(1)}, ...), condition=%wide.region_11.12_spmd, body=%wide.region_8.11_spmd.sunk | while | flops 2181298176 | bytes 59606612 | solution.py:44
  82.8 1.1 dynamic-slice_bitcast_fusion.2
  84.2 9.1 %multiply_reduce_fusion.3 = (f32[2048]{0:T(1024)S(1)}, f32[2048,2048]{0,1:T(8,128)}) fusion(bf16[2048,128]{1,0:T(8,128)(2,1)S(1)} %squeeze.29, bf16[4,2048,128]{2,1,0:T(8,128)(2,1)} %get-tuple-element.283, s32[]{:T(128)} %get-tuple-element.272), kind=kOutput, calls=%fused_computation.5.clone.1 | convolution fusion | flops 1082128384 | bytes 17834496 | tf_op jit(solution)/shard_map/while/body/eval_jaxpr/while/body/eval_jaxpr/dot_general | solution.py:10
  93.3 8.5 %fusion.54 = f32[2048]{0:T(1024)S(1)} fusion(f32[2048,2048]{0,1:T(8,128)} %get-tuple-element.254, f32[2048]{0:T(1024)S(1)} %get-tuple-element.255), kind=kLoop, calls=%fused_computation.6.clone.1 | loop fusion | flops 12580864 | bytes 16793600 | tf_op jit(solution)/shard_map/while/body/eval_jaxpr/while/body/eval_jaxpr/reduce_sum | solution.py:15
  102.6 7.4 %fusion.55 = f32[2048,128]{1,0:T(8,128)S(1)} fusion(f32[2048,2048]{0,1:T(8,128)} %get-tuple-element.254, f32[2048]{0:T(1024)S(1)} %get-tuple-element.255, f32[2048]{0:T(1024)S(1)} %fusion.54, bf16[4,2048,128]{2,1,0:T(8,128)(2,1)} %get-tuple-element.284, s32[]{:T(128)} %get-tuple-element.272), kind=kOutput, calls=%fused_computation.9.clone.1 | convolution fusion | flops 1086586880 | bytes 18366976 | tf_op jit(solution)/shard_map/while/body/eval_jaxpr/while/body/eval_jaxpr/dot_general | solution.py:17
  110.2 1.1 bitcast_dynamic-update-slice_fusion.2
  111.3 1.1 dynamic-slice_bitcast_fusion.2
  112.7 9.1 %multiply_reduce_fusion.3 = (f32[2048]{0:T(1024)S(1)}, f32[2048,2048]{0,1:T(8,128)}) fusion(bf16[2048,128]{1,0:T(8,128)(2,1)S(1)} %squeeze.29, bf16[4,2048,128]{2,1,0:T(8,128)(2,1)} %get-tuple-element.283, s32[]{:T(128)} %get-tuple-element.272), kind=kOutput, calls=%fused_computation.5.clone.1 | convolution fusion | flops 1082128384 | bytes 17834496 | tf_op jit(solution)/shard_map/while/body/eval_jaxpr/while/body/eval_jaxpr/dot_general | solution.py:10
  121.8 8.5 %fusion.54 = f32[2048]{0:T(1024)S(1)} fusion(f32[2048,2048]{0,1:T(8,128)} %get-tuple-element.254, f32[2048]{0:T(1024)S(1)} %get-tuple-element.255), kind=kLoop, calls=%fused_computation.6.clone.1 | loop fusion | flops 12580864 | bytes 16793600 | tf_op jit(solution)/shard_map/while/body/eval_jaxpr/while/body/eval_jaxpr/reduce_sum | solution.py:15
  131.1 7.4 %fusion.55 = f32[2048,128]{1,0:T(8,128)S(1)} fusion(f32[2048,2048]{0,1:T(8,128)} %get-tuple-element.254, f32[2048]{0:T(1024)S(1)} %get-tuple-element.255, f32[2048]{0:T(1024)S(1)} %fusion.54, bf16[4,2048,128]{2,1,0:T(8,128)(2,1)} %get-tuple-element.284, s32[]{:T(128)} %get-tuple-element.272), kind=kOutput, calls=%fused_computation.9.clone.1 | convolution fusion | flops 1086586880 | bytes 18366976 | tf_op jit(solution)/shard_map/while/body/eval_jaxpr/while/body/eval_jaxpr/dot_general | solution.py:17
  138.7 1.2 bitcast_dynamic-update-slice_fusion.2
  139.9 1.1 dynamic-slice_bitcast_fusion.2
  141.3 9.1 %multiply_reduce_fusion.3 = (f32[2048]{0:T(1024)S(1)}, f32[2048,2048]{0,1:T(8,128)}) fusion(bf16[2048,128]{1,0:T(8,128)(2,1)S(1)} %squeeze.29, bf16[4,2048,128]{2,1,0:T(8,128)(2,1)} %get-tuple-element.283, s32[]{:T(128)} %get-tuple-element.272), kind=kOutput, calls=%fused_computation.5.clone.1 | convolution fusion | flops 1082128384 | bytes 17834496 | tf_op jit(solution)/shard_map/while/body/eval_jaxpr/while/body/eval_jaxpr/dot_general | solution.py:10
  150.4 8.5 %fusion.54 = f32[2048]{0:T(1024)S(1)} fusion(f32[2048,2048]{0,1:T(8,128)} %get-tuple-element.254, f32[2048]{0:T(1024)S(1)} %get-tuple-element.255), kind=kLoop, calls=%fused_computation.6.clone.1 | loop fusion | flops 12580864 | bytes 16793600 | tf_op jit(solution)/shard_map/while/body/eval_jaxpr/while/body/eval_jaxpr/reduce_sum | solution.py:15
  159.7 7.4 %fusion.55 = f32[2048,128]{1,0:T(8,128)S(1)} fusion(f32[2048,2048]{0,1:T(8,128)} %get-tuple-element.254, f32[2048]{0:T(1024)S(1)} %get-tuple-element.255, f32[2048]{0:T(1024)S(1)} %fusion.54, bf16[4,2048,128]{2,1,0:T(8,128)(2,1)} %get-tuple-element.284, s32[]{:T(128)} %get-tuple-element.272), kind=kOutput, calls=%fused_computation.9.clone.1 | convolution fusion | flops 1086586880 | bytes 18366976 | tf_op jit(solution)/shard_map/while/body/eval_jaxpr/while/body/eval_jaxpr/dot_general | solution.py:17
  167.3 1.1 bitcast_dynamic-update-slice_fusion.2
  168.4 1.1 dynamic-slice_bitcast_fusion.2
  169.8 9.1 %multiply_reduce_fusion.3 = (f32[2048]{0:T(1024)S(1)}, f32[2048,2048]{0,1:T(8,128)}) fusion(bf16[2048,128]{1,0:T(8,128)(2,1)S(1)} %squeeze.29, bf16[4,2048,128]{2,1,0:T(8,128)(2,1)} %get-tuple-element.283, s32[]{:T(128)} %get-tuple-element.272), kind=kOutput, calls=%fused_computation.5.clone.1 | convolution fusion | flops 1082128384 | bytes 17834496 | tf_op jit(solution)/shard_map/while/body/eval_jaxpr/while/body/eval_jaxpr/dot_general | solution.py:10
  178.9 8.5 %fusion.54 = f32[2048]{0:T(1024)S(1)} fusion(f32[2048,2048]{0,1:T(8,128)} %get-tuple-element.254, f32[2048]{0:T(1024)S(1)} %get-tuple-element.255), kind=kLoop, calls=%fused_computation.6.clone.1 | loop fusion | flops 12580864 | bytes 16793600 | tf_op jit(solution)/shard_map/while/body/eval_jaxpr/while/body/eval_jaxpr/reduce_sum | solution.py:15
  188.2 7.4 %fusion.55 = f32[2048,128]{1,0:T(8,128)S(1)} fusion(f32[2048,2048]{0,1:T(8,128)} %get-tuple-element.254, f32[2048]{0:T(1024)S(1)} %get-tuple-element.255, f32[2048]{0:T(1024)S(1)} %fusion.54, bf16[4,2048,128]{2,1,0:T(8,128)(2,1)} %get-tuple-element.284, s32[]{:T(128)} %get-tuple-element.272), kind=kOutput, calls=%fused_computation.9.clone.1 | convolution fusion | flops 1086586880 | bytes 18366976 | tf_op jit(solution)/shard_map/while/body/eval_jaxpr/while/body/eval_jaxpr/dot_general | solution.py:17
  195.8 1.1 bitcast_dynamic-update-slice_fusion.2
  197.4 14.9 %all_to_all.33 = f32[64,1,128]{2,1,0:T(1,128)S(1)} all-to-all(f32[64,1,128]{2,1,0:T(1,128)S(1)} %reshape.210), channel_id=1, replica_groups=mesh['ctx'=64,'head'=4] {'ctx'}, dimensions={0} | all-to-all | bytes 65536 | tf_op jit(solution)/shard_map/all_to_all | solution.py:74
  212.3 5.8 %all-to-all-start.2 = ((f32[4,64,8,512]{3,2,0,1:T(8,128)}), f32[4,64,8,512]{3,2,0,1:T(8,128)}, u32[]{:S(2)}, u32[]{:S(2)}) async-start(f32[4,64,8,512]{3,2,0,1:T(8,128)} %get-tuple-element.97), calls=%async_computation.2 | async-start | bytes 8388608 | tf_op jit(solution)/shard_map/all_to_all | solution.py:73
  218.4 4.4 %while.31 = (s32[]{:T(128)}, f32[4,128,512]{2,1,0:T(8,128)S(1)}, f32[4,128,4]{2,1,0:T(8,128)S(1)}, bf16[4,128,512]{2,1,0:T(8,128)(2,1)S(1)}, bf16[4,128,128]{2,1...) while((s32[]{:T(128)}, f32[4,128,512]{2,1,0:T(8,128)S(1)}, ...), condition=%wide.region_3.4_spmd.clone, body=%wide.region_0.3_spmd.clone.sunk | while | flops 34078208 | bytes 3248233 | solution.py:90
  223.3 1.4 reshape.170
  225.3 0.7 reduce.6
  226.6 1.6 copy.146
  228.2 9.9 %gather_fusion = f32[1536,4]{1,0:T(8,128)S(1)} fusion(f32[4,512,4]{2,1,0:T(8,128)S(1)} %bitcast.82, s32[1536]{0:T(1024)S(1)} %reshape.178), kind=kCustom, calls=%fused_computation | custom fusion | bytes 61440 | tf_op jit(solution)/shard_map/vmap()/gather | solution.py:96
  238.4 0.9 reshape.181
  240.1 1.3 copy.152
  241.6 72.5 %all-to-all-done.2 = f32[4,64,8,512]{3,2,0,1:T(8,128)} async-done(((f32[4,64,8,512]{3,2,0,1:T(8,128)}), f32[4,64,8,512]{3,2,0,1:T(8,128)}, u32[]{:S(2)}, u32[]{:S(2)}) %all-to-all-start.2) | async-done | bytes 4194336 | tf_op jit(solution)/shard_map/all_to_all | solution.py:73
  314.1 4.8 %copy.180 = f32[4,64,8,512]{3,2,1,0:T(8,128)} copy(f32[4,64,8,512]{3,2,0,1:T(8,128)} %all-to-all-done.2) | data formatting | bytes 8388608 | tf_op jit(solution)/shard_map/all_to_all | solution.py:73
  318.8 18.8 %gather_fusion.1 = f32[1536,512]{1,0:T(8,128)S(1)} fusion(f32[4,512,512]{2,1,0:T(8,128)} %bitcast.81, s32[1536]{0:T(1024)S(1)} %reshape.178), kind=kCustom, calls=%fused_computation.1 | custom fusion | bytes 6303744 | tf_op jit(solution)/shard_map/vmap()/gather | solution.py:96
  337.7 2.7 reshape.172
  340.4 5.9 %fusion.28 = f32[4,128,4,128]{3,2,1,0:T(4,128)S(1)} fusion(f32[4,128,3,4,128]{4,3,2,1,0:T(4,128)} %reshape.172, f32[4,128,1,4,128]{4,3,2,1,0:T(4,128)} %bitcast.87, f32[4,128,4,4]{3,2,1,0:T(4,128)} %copy.152), kind=kLoop, calls=%fused_computation.40 | loop fusion | flops 2883584 | bytes 5275648 | tf_op jit(solution)/shard_map/reduce_sum | solution.py:112
  346.3 0.7 divide_convert_fusion
  347.6 12.6 %all_to_all.34 = bf16[128,4,512]{2,1,0:T(4,128)(2,1)S(1)} all-to-all(bf16[128,4,512]{2,1,0:T(4,128)(2,1)S(1)} %bitcast.89), channel_id=1, replica_groups=mesh['ctx'=64,'head'=4] {'head'}, dimensions={0} | all-to-all | bytes 1048576 | tf_op jit(solution)/shard_map/all_to_all | solution.py:116
  360.4 1.1 copy.161
  (118 shorter events, 15.5 us)
Async XLA Ops:
  18.3 13.3 %copy-start = (bf16[2048,4,128]{2,1,0:T(4,128)(2,1)S(1)}, bf16[2048,4,128]{2,1,0:T(4,128)(2,1)}, u32[]{:S(2)}) copy-start(bf16[2048,4,128]{2,1,0:T(4,128)(2,1)} %param.13) | copy-start | bytes 6291460
  18.3 64.5 %all-to-all-start = ((bf16[4,64,8,512]{3,2,0,1:T(8,128)(2,1)}), bf16[4,64,8,512]{3,2,0,1:T(8,128)(2,1)}, u32[]{:S(2)}, u32[]{:S(2)}) async-start(bf16[4,64,8,512]{3,2,0,1:T(8,128)(2,1)} %copy.141), calls=%async_computation | async-start | bytes 4194304 | tf_op jit(solution)/shard_map/all_to_all | solution.py:70
  212.3 5.9 %copy-start.3 = (s32[1,128]{1,0:T(1,128)S(1)}, s32[1,128]{1,0:T(1,128)}, u32[]{:S(2)}) copy-start(s32[1,128]{1,0:T(1,128)} %param.17) | copy-start | bytes 1540
  212.3 6.0 %copy-start.1 = (bf16[128,4,128]{2,1,0:T(4,128)(2,1)S(1)}, bf16[128,4,128]{2,1,0:T(4,128)(2,1)}, u32[]{:S(2)}) copy-start(bf16[128,4,128]{2,1,0:T(4,128)(2,1)} %param.15) | copy-start | bytes 393220
  212.3 6.0 %copy-start.2 = (bf16[128,4,128]{2,1,0:T(4,128)(2,1)S(1)}, bf16[128,4,128]{2,1,0:T(4,128)(2,1)}, u32[]{:S(2)}) copy-start(bf16[128,4,128]{2,1,0:T(4,128)(2,1)} %param.14) | copy-start | bytes 393220
  212.3 101.8 %all-to-all-start.2 = ((f32[4,64,8,512]{3,2,0,1:T(8,128)}), f32[4,64,8,512]{3,2,0,1:T(8,128)}, u32[]{:S(2)}, u32[]{:S(2)}) async-start(f32[4,64,8,512]{3,2,0,1:T(8,128)} %get-tuple-element.97), calls=%async_computation.2 | async-start | bytes 8388608 | tf_op jit(solution)/shard_map/all_to_all | solution.py:73
where the time goes:
time: 363 us; the launch traced here: 362 us
  waiting for transfers between devices  119 us (33%)
  local copies, waits for them, and re-layouts  81.7 us (23%)
  matrix products  67.8 us (19%)
  other arithmetic  44.9 us (12%)
  blocking collectives  27.5 us (8%)
  starting transfers between devices  19.1 us (5%)
    all_to_all x1, waiting for transfers between devices, local(): lax.all_to_all(far_out, 'ctx', split_axis=1, concat_axis=1, tiled=True)  72.5 us
    all_to_all x1, waiting for transfers between devices, local(): lax.all_to_all(outbound, 'ctx', split_axis=1, concat_axis=1, tiled=True)  47 us
    dot_general x8, matrix products, attend(): jnp.dot(query_rows, key_rows.T, preferred_element_type=jnp.float32)  37.2 us
    reduce_sum x8, other arithmetic, attend(): denominator = jnp.sum(weights, axis=1, keepdims=True)  34.4 us
    gather x7, local copies, waits for them, and re-layouts, take_rows(): return source_rows[indices]  30.6 us
    dot_general x8, matrix products, attend(): jnp.dot(weights.astype(jnp.bfloat16), value_rows, preferred_element_type=...  30.6 us
    all_to_all x1, blocking collectives, local(): lax.all_to_all(far_lse, 'ctx', split_axis=1, concat_axis=1, tiled=True)  14.9 us
    all_to_all x1, starting transfers between devices, local(): lax.all_to_all(outbound, 'ctx', split_axis=1, concat_axis=1, tiled=True)  13.3 us
  transfers between devices with their start and end apart: 2, of which 2 were waited for; matrix products, arithmetic and copies ran while one was open for 7% of the time, Pallas kernels for 0%

commit v1 on v0

v1 whole, which is shorter than its diff:
```python
import math

import jax
import jax.numpy as jnp
from jax import lax
from jax.experimental import pallas as pl
from jax.experimental.pallas import tpu as pltpu
from jax.sharding import PartitionSpec as P

CHUNKS = 2
LSE_ROWS = 8
VMEM_LIMIT = 56 * 1024 * 1024
TILE_SOURCES = 8


def whole():
    return pl.BlockSpec(memory_space=pltpu.VMEM)


def slot_of(chosen, sources, capacity):
    tokens = chosen.shape[0]
    block_ids = lax.broadcasted_iota(jnp.int32, (tokens, sources), 1)
    hits = [(chosen[:, j : j + 1] == block_ids).astype(jnp.float32) for j in range(3)]
    occupied = (hits[0] + hits[1] + hits[2]).astype(jnp.bfloat16)
    row = lax.broadcasted_iota(jnp.int32, (tokens, tokens), 0)
    column = lax.broadcasted_iota(jnp.int32, (tokens, tokens), 1)
    before = (column < row).astype(jnp.bfloat16)
    earlier = jnp.dot(before, occupied, preferred_element_type=jnp.float32)
    ranks = [jnp.sum(hit * earlier, axis=1, keepdims=True).astype(jnp.int32) for hit in hits]
    return hits, ranks


def slot_hits(chosen, ranks, sources, capacity):
    tokens = chosen.shape[0]
    slot_ids = lax.broadcasted_iota(jnp.int32, (tokens, sources * capacity), 1)
    return [(chosen[:, j : j + 1] * capacity + ranks[j]) == slot_ids for j in range(3)]


def dispatch_kernel(sources, capacity, heads, width, q_ref, choices_ref, *out_refs):
    groups = choices_ref.shape[0]
    per_chunk = groups // len(out_refs)
    row_width = heads * width
    for g in range(groups):
        chosen = choices_ref[g]
        _, ranks = slot_of(chosen, sources, capacity)
        hit = slot_hits(chosen, ranks, sources, capacity)
        pick = (hit[0] | hit[1] | hit[2]).astype(jnp.float32).T.astype(jnp.bfloat16)
        rows = q_ref[:, g * row_width : (g + 1) * row_width]
        filled = jnp.dot(pick, rows, preferred_element_type=jnp.float32)
        filled = filled.reshape(sources, capacity, row_width)
        by_head = [filled[:, :, h * width : (h + 1) * width] for h in range(heads)]
        out_refs[g // per_chunk][:, g % per_chunk] = jnp.concatenate(by_head, axis=1).astype(
            jnp.bfloat16
        )


def far_kernel(first_group, scale, last, q_ref, k_ref, v_ref, *refs):
    if last:
        lse_in_ref, out_ref, lse_ref, wide_ref = refs
    else:
        out_ref, lse_ref, wide_ref = refs
    g = pl.program_id(0)
    sources, _, per_source, width = q_ref.shape
    keys = k_ref.shape[0]
    wide_ref[:, :width] = v_ref[...]
    wide_ref[:, width:] = jnp.ones((keys, width), jnp.bfloat16)

    @pl.when(g == 0)
    def _():
        lse_ref[...] = lse_in_ref[...] if last else jnp.zeros_like(lse_ref)

    rows = TILE_SOURCES * per_source
    fold = scale * math.log2(math.e)

    def tile(start):
        q = q_ref[pl.ds(start, TILE_SOURCES), 0].reshape(rows, width)
        scores = lax.dot_general(
            q, k_ref[...], (((1,), (1,)), ((), ())), preferred_element_type=jnp.float32
        )
        highest = jnp.max(scores, axis=1, keepdims=True)
        weights = jnp.exp2((scores - highest) * fold).astype(jnp.bfloat16)
        both = jnp.dot(weights, wide_ref[...], preferred_element_type=jnp.float32)
        total = both[:, width:]
        blended = both[:, :width] / total
        lse = highest * scale + jnp.log(total)
        return blended, lse

    lane = lax.broadcasted_iota(jnp.int32, (TILE_SOURCES, per_source, width), 2)
    index = lax.broadcasted_iota(jnp.int32, (TILE_SOURCES, per_source, width), 1)
    mine = lane == index + (first_group + g) * per_source

    def step(i, carry):
        starts = [pl.multiple_of((2 * i + n) * TILE_SOURCES, TILE_SOURCES) for n in range(2)]
        results = [tile(start) for start in starts]
        for start, (blended, lse) in zip(starts, results):
            at = pl.ds(start, TILE_SOURCES)
            out_ref[at, pl.ds(pl.multiple_of(g * per_source, per_source), per_source), :] = (
                blended.reshape(TILE_SOURCES, per_source, width).astype(jnp.bfloat16)
            )
            spread = jnp.where(mine, lse.reshape(TILE_SOURCES, per_source, width), 0.0)
            lse_ref[at, :] += jnp.sum(spread, axis=1)
        return carry

    lax.fori_loop(0, sources // (2 * TILE_SOURCES), step, 0)

    if last:

        @pl.when(g == pl.num_programs(0) - 1)
        def _():
            table = lse_ref[...]
            coarse = table.astype(jnp.bfloat16).astype(jnp.float32)
            fine = table - coarse
            rest = jnp.zeros((sources, LSE_ROWS - 2, width), jnp.float32)
            extra = jnp.concatenate([coarse[:, None, :], fine[:, None, :], rest], axis=1)
            out_ref[:, pl.num_programs(0) * per_source :, :] = extra.astype(jnp.bfloat16)


def near_kernel(sources, capacity, heads, width, scale, q_ref, k_ref, v_ref, choices_ref,
                row_pos_ref, col_pos_ref, out_ref, lse_ref, pick_ref, block_ref, rank_ref):
    groups, tokens, _ = choices_ref.shape
    allowed = row_pos_ref[...] <= col_pos_ref[...]
    for g in range(groups):
        chosen = choices_ref[g]
        hits, ranks = slot_of(chosen, sources, capacity)
        slots = slot_hits(chosen, ranks, sources, capacity)
        lane = lax.broadcasted_iota(jnp.int32, (tokens, heads * groups * capacity), 1)
        for j in range(3):
            at = slice(j * tokens, (j + 1) * tokens)
            pick_ref[g, at] = slots[j].astype(jnp.float32).astype(jnp.bfloat16)
            block_ref[g, at] = hits[j].astype(jnp.bfloat16)
            in_group = (lane >= g * heads * capacity) & (lane < (g + 1) * heads * capacity)
            here = in_group & (lane % capacity == ranks[j])
            rank_ref[g, at] = here.astype(jnp.float32).astype(jnp.bfloat16)
        keys = k_ref[:, g * width : (g + 1) * width]
        values = v_ref[:, g * width : (g + 1) * width]
        for h in range(heads):
            at = slice((g * heads + h) * width, (g * heads + h + 1) * width)
            scores = lax.dot_general(
                q_ref[:, at], keys, (((1,), (1,)), ((), ())), preferred_element_type=jnp.float32
            )
            scores = jnp.where(allowed, scores * scale, -jnp.inf)
            highest = jnp.max(scores, axis=1, keepdims=True)
            weights = jnp.exp(scores - highest)
            total = jnp.sum(weights, axis=1, keepdims=True)
            blended = jnp.dot(
                weights.astype(jnp.bfloat16), values, preferred_element_type=jnp.float32
            )
            out_ref[:, at] = blended / total
            lse_ref[:, at] = jnp.broadcast_to(highest + jnp.log(total), (tokens, width))


def merge_kernel(capacity, heads, width, near_ref, near_lse_ref, pick_ref, block_ref, rank_ref,
                 *refs):
    back_refs, out_ref = refs[:-1], refs[-1]
    groups = pick_ref.shape[0]
    per_chunk = groups // len(back_refs)
    sources = back_refs[0].shape[0]
    tokens = near_ref.shape[0]
    per_source = heads * capacity
    row_width = heads * width
    extra = back_refs[-1][:, per_chunk * per_source :, :].astype(jnp.float32)
    coarse = extra[:, 0, :].astype(jnp.bfloat16)
    fine = extra[:, 1, :].astype(jnp.bfloat16)
    lane = lax.broadcasted_iota(jnp.int32, (groups * per_source, row_width), 0)
    column = lax.broadcasted_iota(jnp.int32, (groups * per_source, row_width), 1)
    spread = ((lane // capacity) % heads == column // width).astype(jnp.float32)
    spread = spread.astype(jnp.bfloat16)
    for g in range(groups):
        back_ref = back_refs[g // per_chunk]
        first = (g % per_chunk) * per_source
        rows = back_ref[:, first : first + per_source, :].astype(jnp.float32)
        by_head = [
            rows[:, h * capacity : (h + 1) * capacity, :].reshape(sources * capacity, width)
            for h in range(heads)
        ]
        table = jnp.concatenate(by_head, axis=1).astype(jnp.bfloat16)
        got = jnp.dot(pick_ref[g], table, preferred_element_type=jnp.float32)
        lse = jnp.zeros((3 * tokens, row_width), jnp.float32)
        for part in (coarse, fine):
            picked = jnp.dot(block_ref[g], part, preferred_element_type=jnp.float32)
            picked = picked.astype(jnp.bfloat16) * rank_ref[g]
            lse += jnp.dot(picked, spread, preferred_element_type=jnp.float32)
        at = slice(g * row_width, (g + 1) * row_width)
        all_lse = [near_lse_ref[:, at]] + [lse[j * tokens : (j + 1) * tokens] for j in range(3)]
        all_out = [near_ref[:, at]] + [got[j * tokens : (j + 1) * tokens] for j in range(3)]
        highest = all_lse[0]
        for item in all_lse[1:]:
            highest = jnp.maximum(highest, item)
        top = jnp.zeros((tokens, row_width), jnp.float32)
        bottom = jnp.zeros((tokens, row_width), jnp.float32)
        for item, part in zip(all_lse, all_out):
            weight = jnp.exp(item - highest)
            top += weight * part
            bottom += weight
        out_ref[g] = (top / bottom).astype(jnp.bfloat16)


def local(queries, hist_keys, hist_values, own_keys, own_values, choices, positions):
    sources = lax.axis_size("ctx")
    tokens, groups, row_width = queries.shape
    keys, _, width = hist_keys.shape
    heads = row_width // width
    capacity = 4 * tokens // sources
    per_source = heads * capacity
    scale = width ** (-0.5)
    per_chunk = groups // CHUNKS
    params = pltpu.CompilerParams(vmem_limit_bytes=VMEM_LIMIT)
    bf16, f32 = jnp.bfloat16, jnp.float32

    flat_queries = queries.reshape(tokens, groups * row_width)
    outbound = pl.pallas_call(
        lambda *refs: dispatch_kernel(sources, capacity, heads, width, *refs),
        out_shape=[jax.ShapeDtypeStruct((sources, per_chunk, per_source, width), bf16)] * CHUNKS,
        in_specs=[whole()] * 2,
        out_specs=[whole()] * CHUNKS,
        compiler_params=params,
        name="dispatch",
    )(flat_queries, choices)
    received = [lax.all_to_all(item, "ctx", 0, 0, tiled=True) for item in outbound]

    flat_keys = hist_keys.reshape(keys, groups * width)
    flat_values = hist_values.reshape(keys, groups * width)

    def far(chunk, lse_table):
        last = chunk == CHUNKS - 1
        first_group = chunk * per_chunk
        rows = per_chunk * per_source + (LSE_ROWS if last else 0)
        work = per_chunk * sources * per_source * keys
        return pl.pallas_call(
            lambda *refs: far_kernel(first_group, scale, last, *refs),
            grid=(per_chunk,),
            in_specs=[
                pl.BlockSpec((sources, 1, per_source, width), lambda g: (0, g, 0, 0)),
                pl.BlockSpec((keys, width), lambda g: (0, first_group + g)),
                pl.BlockSpec((keys, width), lambda g: (0, first_group + g)),
            ]
            + ([pl.BlockSpec((sources, groups * per_source), lambda g: (0, 0))] if last else []),
            out_specs=[
                pl.BlockSpec((sources, rows, width), lambda g: (0, 0, 0)),
                pl.BlockSpec((sources, groups * per_source), lambda g: (0, 0)),
            ],
            out_shape=[
                jax.ShapeDtypeStruct((sources, rows, width), bf16),
                jax.ShapeDtypeStruct((sources, groups * per_source), f32),
            ],
            scratch_shapes=[pltpu.VMEM((keys, 2 * width), bf16)],
            compiler_params=params,
            cost_estimate=pl.CostEstimate(
                flops=6 * work * width, transcendentals=work, bytes_accessed=4 * work // keys * width
            ),
            name="far",
        )(received[chunk], flat_keys, flat_values, *((lse_table,) if last else ()))

    back = []
    lse_table = jnp.zeros((sources, groups * per_source), f32)
    for chunk in range(CHUNKS):
        out, lse_table = far(chunk, lse_table)
        back.append(lax.all_to_all(out, "ctx", 0, 0, tiled=True))

    flat = (tokens, groups * row_width)
    near = pl.pallas_call(
        lambda *refs: near_kernel(sources, capacity, heads, width, scale, *refs),
        out_shape=[
            jax.ShapeDtypeStruct(flat, f32),
            jax.ShapeDtypeStruct(flat, f32),
            jax.ShapeDtypeStruct((groups, 3 * tokens, sources * capacity), bf16),
            jax.ShapeDtypeStruct((groups, 3 * tokens, sources), bf16),
            jax.ShapeDtypeStruct((groups, 3 * tokens, groups * per_source), bf16),
        ],
        in_specs=[whole()] * 6,
        out_specs=[whole()] * 5,
        compiler_params=params,
        cost_estimate=pl.CostEstimate(
            flops=4 * tokens * tokens * groups * row_width,
            transcendentals=tokens * tokens * groups * heads,
            bytes_accessed=16 * tokens * groups * row_width,
        ),
        name="near",
    )(
        flat_queries,
        own_keys.reshape(tokens, groups * width),
        own_values.reshape(tokens, groups * width),
        choices,
        positions,
        positions.reshape(tokens, 1),
    )

    merged = pl.pallas_call(
        lambda *refs: merge_kernel(capacity, heads, width, *refs),
        out_shape=jax.ShapeDtypeStruct((groups, tokens, row_width), bf16),
        in_specs=[whole()] * (5 + CHUNKS),
        out_specs=whole(),
        compiler_params=params,
        name="merge",
    )(*near, *back)
    merged = jnp.transpose(merged, (1, 0, 2))
    return lax.all_to_all(merged, "head", split_axis=0, concat_axis=1, tiled=True)


def solution(mesh):
    in_specs = (
        P("ctx", "head", None),
        P("ctx", "head", None),
        P("ctx", "head", None),
        P("ctx", "head", None),
        P("ctx", "head", None),
        P("head", "ctx", None),
        P("ctx", None),
    )
    out_specs = P(("ctx", "head"), None, None)
    return jax.shard_map(local, mesh=mesh, in_specs=in_specs, out_specs=out_specs, check_vma=False)
```

time: 363 us -> 181 us (0.50)
  waiting for transfers between devices: 119 us -> 38.5 us
  local copies, waits for them, and re-layouts: 81.7 us -> 13 us
  matrix products: 67.8 us -> 0 us
  Pallas kernels: 0 us -> 55.4 us
  other arithmetic: 44.9 us -> 0 us
  blocking collectives: 27.5 us -> 55.1 us
    all_to_all x2 -> x3, waiting for transfers between devices: 119 us -> 38.5 us  [the longest x2 32.9 us: local(): back.append(lax.all_to_all(out, 'ctx', 0, 0, tiled=True))]
    dot_general x16 -> x0, matrix products: 67.8 us -> none  [the longest x8 37.2 us: attend(): jnp.dot(query_rows, key_rows.T, preferred_element_type=jnp.float32)]
    pallas_call x0 -> x5, Pallas kernels: none -> 55.4 us  [the longest x2 37.4 us: far(): pl.pallas_call(lambda *refs: far_kernel(first_group, scale, last, *refs),...]
    reduce_sum x12 -> x0, other arithmetic: 40.5 us -> none  [the longest x8 34.4 us: attend(): denominator = jnp.sum(weights, axis=1, keepdims=True)]
    gather x7 -> x0, local copies, waits for them, and re-layouts: 30.6 us -> none  [take_rows(): return source_rows[indices]]
    all_to_all x1, blocking collectives: 14.9 us -> 41.8 us  [local(): lax.all_to_all(item, 'ctx', 0, 0, tiled=True)]
    unnamed x15 -> x16, local copies, waits for them, and re-layouts: 11.5 us -> 4.56 us
    all_to_all x3 -> x0, local copies, waits for them, and re-layouts: 6.82 us -> none  [the longest x1 4.75 us: local(): lax.all_to_all(far_out, 'ctx', split_axis=1, concat_axis=1, tiled=True)]
  transfers between devices with their start and end apart: 2 -> 3, of which waited for: 2 -> 3; matrix products, arithmetic and copies ran while one was open for 7% -> 3% of each run, Pallas kernels for 0% -> 24%
where the time goes in v1:
time: 181 us
  Pallas kernels  55.4 us (31%)
  blocking collectives  55.1 us (30%)
  waiting for transfers between devices  38.5 us (21%)
  starting transfers between devices  18.6 us (10%)
  local copies, waits for them, and re-layouts  13 us (7%)
    all_to_all x1, blocking collectives, local(): lax.all_to_all(item, 'ctx', 0, 0, tiled=True)  41.8 us
    pallas_call x2, Pallas kernels, far(): pl.pallas_call(lambda *refs: far_kernel(first_group, scale, last, *refs),...  37.4 us
    all_to_all x2, waiting for transfers between devices, local(): back.append(lax.all_to_all(out, 'ctx', 0, 0, tiled=True))  32.9 us
    all_to_all x1, blocking collectives, local(): lax.all_to_all(merged, 'head', split_axis=0, concat_axis=1, tiled=True)  13.3 us
    all_to_all x2, starting transfers between devices, local(): back.append(lax.all_to_all(out, 'ctx', 0, 0, tiled=True))  12.4 us
    pallas_call x1, Pallas kernels, local(): pl.pallas_call(lambda *refs: near_kernel(sources, capacity, heads, width,...  6.72 us
    pallas_call x1, Pallas kernels, local(): pl.pallas_call(lambda *refs: merge_kernel(capacity, heads, width, *refs),...  6.71 us
    all_to_all x1, starting transfers between devices, local(): lax.all_to_all(item, 'ctx', 0, 0, tiled=True)  6.19 us
  transfers between devices with their start and end apart: 3, of which 3 were waited for; matrix products, arithmetic and copies ran while one was open for 3% of the time, Pallas kernels for 24%

profile of v1, /device:TPU:1, one launch (start us, length us, event | category | flops | bytes accessed | tf_op | source)
XLA Modules:
  0.0 180.6 jit_solution(17984355719579193985)
XLA Ops:
  0.0 1.9 %copy.17 = bf16[16,8,4,512]{3,1,2,0:T(8,128)(2,1)} copy(bf16[16,8,4,512]{3,2,1,0:T(4,128)(2,1)} %bitcast.25) | data formatting | bytes 1048576
  1.9 1.5 copy.12.refs_3_.refs_1_
  3.5 4.5 %dispatch.1 = (bf16[64,2,32,128]{3,2,1,0:T(8,128)(2,1)}, bf16[64,2,32,128]{3,2,1,0:T(8,128)(2,1)}) custom-call(bf16[128,2048]{1,0:T(8,128)(2,1)} %bitcast.19, s32[4,128,3]{2,1,0:T(8,128)} %copy.12.refs_3_.refs_1_), custom_call_target="tpu_custom_call" | custom-call | tf_op jit(solution)/shard_map/dispatch/pallas_call | solution.py:211
  8.0 0.0 copy-start.2
  8.0 41.8 %all_to_all.38.refs_0_ = bf16[64,2,32,128]{3,2,1,0:T(8,128)(2,1)} all-to-all(bf16[64,2,32,128]{3,2,1,0:T(8,128)(2,1)} %get-tuple-element.20), channel_id=1, replica_groups=mesh['ctx'=64,'head'=4] {'ctx'}, dimensions={0} | all-to-all | bytes 2097152 | tf_op jit(solution)/shard_map/all_to_all | solution.py:219
  49.8 6.2 %all-to-all-start.2 = ((bf16[64,2,32,128]{3,2,1,0:T(8,128)(2,1)}), bf16[64,2,32,128]{3,2,1,0:T(8,128)(2,1)S(1)}, u32[]{:S(2)}, u32[]{:S(2)}) async-start(bf16[64,2,32,128]{3,2,1,0:T(8,128)(2,1)} %get-tuple-element.22), calls=%async_computation.2 | async-start | bytes 2097152 | tf_op jit(solution)/shard_map/all_to_all | solution.py:219
  56.0 0.0 copy-done.2
  56.0 4.3 %copy_bitcast_fusion = (bf16[2048,512]{1,0:T(8,128)(2,1)}, bf16[2048,512]{1,0:T(8,128)(2,1)}) fusion(bf16[256,8,4,128]{3,2,1,0:T(4,128)(2,1)S(1)} %bitcast.23, bf16[256,8,4,128]{3,2,1,0:T(4,128)(2,1)} %bitcast.24), kind=kLoop, calls=%fused_computation | loop fusion | bytes 8388608 | tf_op jit(solution)/shard_map/reshape | solution.py:222
  60.3 18.6 %far.2 = (bf16[64,64,128]{2,1,0:T(8,128)(2,1)}, f32[64,128]{1,0:T(8,128)}) custom-call(bf16[64,2,32,128]{3,2,1,0:T(8,128)(2,1)} %all_to_all.38.refs_0_, bf16[2048,512]{1,0:T(8,128)(2,1)} %get-tuple-element.28.refs_1_, bf16[2048,512]{1,0:T(8,128)(2,1)} %get-tuple-element.27.refs_2_), custom_call_target="tpu_custom_call" | custom-call | flops 6442450944 | bytes 2097152 | tf_op jit(solution)/shard_map/far/pallas_call | solution.py:229
  78.9 5.6 %all-to-all-done.2.refs_0_ = bf16[64,2,32,128]{3,2,1,0:T(8,128)(2,1)S(1)} async-done(((bf16[64,2,32,128]{3,2,1,0:T(8,128)(2,1)}), bf16[64,2,32,128]{3,2,1,0:T(8,128)(2,1)S(1)}, u32[]{:S(2)}, u32[]{:S(2)}) %all-to-all-start.2) | async-done | bytes 1048608 | tf_op jit(solution)/shard_map/all_to_all | solution.py:219
  84.6 0.0 copy-start.3
  84.6 6.2 %all-to-all-start.1 = ((bf16[64,64,128]{2,1,0:T(8,128)(2,1)}), bf16[64,64,128]{2,1,0:T(8,128)(2,1)S(1)}, u32[]{:S(2)}, u32[]{:S(2)}) async-start(bf16[64,64,128]{2,1,0:T(8,128)(2,1)} %get-tuple-element.21), calls=%async_computation.1 | async-start | bytes 2097152 | tf_op jit(solution)/shard_map/all_to_all | solution.py:258
  90.8 0.0 copy-done.3
  90.8 18.8 %far.3 = (bf16[64,72,128]{2,1,0:T(8,128)(2,1)}, f32[64,128]{1,0:T(8,128)}) custom-call(bf16[64,2,32,128]{3,2,1,0:T(8,128)(2,1)} %copy-done.3, bf16[2048,512]{1,0:T(8,128)(2,1)} %get-tuple-element.28.refs_1_, bf16[2048,512]{1,0:T(8,128)(2,1)} %get-tuple-element.27.refs_2_, f32[64,128]{1,0:T(8,128)} %get-tuple-element.23.refs_3_), custom_call_target="tpu_custom_call" | custom-call | flops 6442450944 | bytes 2097152 | tf_op jit(solution)/shard_map/far/pallas_call | solution.py:229
  109.6 0.0 copy-start.6
  109.6 0.0 copy-start.4
  109.6 0.0 copy-start.5
  109.6 9.7 %all-to-all-done.1.refs_5_ = bf16[64,64,128]{2,1,0:T(8,128)(2,1)S(1)} async-done(((bf16[64,64,128]{2,1,0:T(8,128)(2,1)}), bf16[64,64,128]{2,1,0:T(8,128)(2,1)S(1)}, u32[]{:S(2)}, u32[]{:S(2)}) %all-to-all-start.1) | async-done | bytes 1048608 | tf_op jit(solution)/shard_map/all_to_all | solution.py:258
  119.3 0.0 copy-start.1
  119.3 6.2 %all-to-all-start.3 = ((bf16[64,72,128]{2,1,0:T(8,128)(2,1)}), bf16[64,72,128]{2,1,0:T(8,128)(2,1)S(1)}, u32[]{:S(2)}, u32[]{:S(2)}) async-start(bf16[64,72,128]{2,1,0:T(8,128)(2,1)} %get-tuple-element.24), calls=%async_computation.3 | async-start | bytes 2359296 | tf_op jit(solution)/shard_map/all_to_all | solution.py:258
  125.5 0.0 copy-done.6
  125.5 0.7 copy.13.refs_5_
  126.3 0.0 copy-done.4
  126.3 0.0 copy-done.5
  126.3 0.7 copy_bitcast_fusion.2
  127.0 6.7 %near.1 = (f32[128,2048]{1,0:T(8,128)}, f32[128,2048]{1,0:T(8,128)}, bf16[4,384,512]{2,1,0:T(8,128)(2,1)}, bf16[4,384,64]{2,1,0:T(8,128)(2,1)}, bf16[4,384,128]{2,1,0:T(8,128)(2,1)}) custom-call(bf16[128,2048]{1,0:T(8,128)(2,1)} %bitcast.20, bf16[128,512]{1,0:T(8,128)(2,1)} %get-tuple-element.26.refs_1_, bf16[128,512]{1,0:T(8,128)(2,1)} %get-tuple-element.25.refs_2_, ...), custom_call_target="tpu_custom_call" | custom-call | flops 134217728 | bytes 4194304 | tf_op jit(solution)/shard_map/near/pallas_call | solution.py:261
  133.7 23.2 %all-to-all-done.3.refs_6_ = bf16[64,72,128]{2,1,0:T(8,128)(2,1)S(1)} async-done(((bf16[64,72,128]{2,1,0:T(8,128)(2,1)}), bf16[64,72,128]{2,1,0:T(8,128)(2,1)S(1)}, u32[]{:S(2)}, u32[]{:S(2)}) %all-to-all-start.3) | async-done | bytes 1179680 | tf_op jit(solution)/shard_map/all_to_all | solution.py:258
  156.9 0.0 copy-start
  156.9 0.0 copy-done.1
  156.9 1.1 copy-done
  157.9 6.7 %merge.1 = bf16[4,128,512]{2,1,0:T(8,128)(2,1)} custom-call(f32[128,2048]{1,0:T(8,128)} %get-tuple-element.15.refs_0_, f32[128,2048]{1,0:T(8,128)} %get-tuple-element.16.refs_1_, bf16[4,384,512]{2,1,0:T(8,128)(2,1)} %get-tuple-element.17.refs_2_, bf16[4,384,64]{2,1,0:T(8,128)(2,1)} %get-tuple-element.18.refs_3_, ...), custom_call_target="tpu_custom_call" | custom-call | tf_op jit(solution)/shard_map/merge/pallas_call | solution.py:288
  164.6 1.4 copy.15
  166.1 13.3 %all_to_all.39 = bf16[128,4,512]{2,1,0:T(4,128)(2,1)S(1)} all-to-all(bf16[128,4,512]{2,1,0:T(4,128)(2,1)S(1)} %copy.15), channel_id=1, replica_groups=mesh['ctx'=64,'head'=4] {'head'}, dimensions={0} | all-to-all | bytes 1048576 | tf_op jit(solution)/shard_map/all_to_all | solution.py:297
  179.4 0.3 copy.16
  179.7 0.9 all_to_all.32
Async XLA Ops:
  8.0 48.0 %copy-start.2 = (bf16[2048,4,128]{2,1,0:T(4,128)(2,1)S(1)}, bf16[2048,4,128]{2,1,0:T(4,128)(2,1)}, u32[]{:S(2)}) copy-start(bf16[2048,4,128]{2,1,0:T(4,128)(2,1)} %param.9) | copy-start | bytes 6291460
  49.8 34.8 %all-to-all-start.2 = ((bf16[64,2,32,128]{3,2,1,0:T(8,128)(2,1)}), bf16[64,2,32,128]{3,2,1,0:T(8,128)(2,1)S(1)}, u32[]{:S(2)}, u32[]{:S(2)}) async-start(bf16[64,2,32,128]{3,2,1,0:T(8,128)(2,1)} %get-tuple-element.22), calls=%async_computation.2 | async-start | bytes 2097152 | tf_op jit(solution)/shard_map/all_to_all | solution.py:219
  84.6 6.2 %copy-start.3 = (bf16[64,2,32,128]{3,2,1,0:T(8,128)(2,1)}, bf16[64,2,32,128]{3,2,1,0:T(8,128)(2,1)S(1)}, u32[]{:S(2)}) copy-start(bf16[64,2,32,128]{3,2,1,0:T(8,128)(2,1)S(1)} %all-to-all-done.2.refs_0_) | copy-start | bytes 3145732
  84.6 34.8 %all-to-all-start.1 = ((bf16[64,64,128]{2,1,0:T(8,128)(2,1)}), bf16[64,64,128]{2,1,0:T(8,128)(2,1)S(1)}, u32[]{:S(2)}, u32[]{:S(2)}) async-start(bf16[64,64,128]{2,1,0:T(8,128)(2,1)} %get-tuple-element.21), calls=%async_computation.1 | async-start | bytes 2097152 | tf_op jit(solution)/shard_map/all_to_all | solution.py:258
  109.6 16.0 %copy-start.6 = (s32[1,128]{1,0:T(1,128)S(1)}, s32[1,128]{1,0:T(1,128)}, u32[]{:S(2)}) copy-start(s32[1,128]{1,0:T(1,128)} %refs_4_.1) | copy-start | bytes 1540
  109.6 16.7 %copy-start.4 = (bf16[128,4,128]{2,1,0:T(4,128)(2,1)S(1)}, bf16[128,4,128]{2,1,0:T(4,128)(2,1)}, u32[]{:S(2)}) copy-start(bf16[128,4,128]{2,1,0:T(4,128)(2,1)} %param.11) | copy-start | bytes 393220
  109.6 16.7 %copy-start.5 = (bf16[128,4,128]{2,1,0:T(4,128)(2,1)S(1)}, bf16[128,4,128]{2,1,0:T(4,128)(2,1)}, u32[]{:S(2)}) copy-start(bf16[128,4,128]{2,1,0:T(4,128)(2,1)} %param.10) | copy-start | bytes 393220
  119.3 37.6 %copy-start.1 = (bf16[64,64,128]{2,1,0:T(8,128)(2,1)}, bf16[64,64,128]{2,1,0:T(8,128)(2,1)S(1)}, u32[]{:S(2)}) copy-start(bf16[64,64,128]{2,1,0:T(8,128)(2,1)S(1)} %all-to-all-done.1.refs_5_) | copy-start | bytes 3145732
  119.3 37.6 %all-to-all-start.3 = ((bf16[64,72,128]{2,1,0:T(8,128)(2,1)}), bf16[64,72,128]{2,1,0:T(8,128)(2,1)S(1)}, u32[]{:S(2)}, u32[]{:S(2)}) async-start(bf16[64,72,128]{2,1,0:T(8,128)(2,1)} %get-tuple-element.24), calls=%async_computation.3 | async-start | bytes 2359296 | tf_op jit(solution)/shard_map/all_to_all | solution.py:258
  156.9 1.1 copy-start

commit v2 on v1

v2 whole, which is shorter than its diff:
```python
import math

import jax
import jax.numpy as jnp
from jax import lax
from jax.experimental import pallas as pl
from jax.experimental.pallas import tpu as pltpu
from jax.sharding import PartitionSpec as P

SPLIT = (3, 1)
LSE_ROWS = 8
KEY_CHUNK = 256
TILES = 4
WIDE_LIMIT = 60 * 1024 * 1024
SMALL_LIMIT = 24 * 1024 * 1024


def whole():
    return pl.BlockSpec(memory_space=pltpu.VMEM)


def columns_of(choices_ref):
    count, groups, tokens = choices_ref.shape
    rows = choices_ref[...].astype(jnp.float32).reshape(count * groups, tokens)
    pad = jnp.zeros((tokens - count * groups, tokens), jnp.float32)
    columns = jnp.concatenate([rows, pad], axis=0).T.astype(jnp.int32)
    return [[columns[:, j * groups + g : j * groups + g + 1] for j in range(count)] for g in range(groups)]


def ranks_of(chosen, sources):
    tokens = chosen[0].shape[0]
    block_ids = lax.broadcasted_iota(jnp.int32, (tokens, sources), 1)
    hits = [(item == block_ids).astype(jnp.float32) for item in chosen]
    occupied = (hits[0] + hits[1] + hits[2]).astype(jnp.bfloat16)
    row = lax.broadcasted_iota(jnp.int32, (tokens, tokens), 0)
    column = lax.broadcasted_iota(jnp.int32, (tokens, tokens), 1)
    before = (column < row).astype(jnp.bfloat16)
    earlier = jnp.dot(before, occupied, preferred_element_type=jnp.float32)
    return [jnp.sum(hit * earlier, axis=1, keepdims=True).astype(jnp.int32) for hit in hits]


def dispatch_kernel(first, sources, capacity, heads, width, q_ref, choices_ref, out_ref):
    tokens = choices_ref.shape[2]
    row_width = heads * width
    chosen = columns_of(choices_ref)
    slot_ids = lax.broadcasted_iota(jnp.int32, (tokens, sources * capacity), 1)
    for i in range(out_ref.shape[1]):
        g = first + i
        hit = None
        for block, rank in zip(chosen[g], ranks_of(chosen[g], sources)):
            mine = block * capacity + rank == slot_ids
            hit = mine if hit is None else hit | mine
        pick = hit.astype(jnp.float32).T.astype(jnp.bfloat16)
        rows = q_ref[:, g * row_width : (g + 1) * row_width]
        filled = jnp.dot(pick, rows, preferred_element_type=jnp.float32)
        filled = filled.reshape(sources, capacity, row_width)
        by_head = [filled[:, :, h * width : (h + 1) * width] for h in range(heads)]
        out_ref[:, i] = jnp.concatenate(by_head, axis=1).astype(jnp.bfloat16)


def far_kernel(first, last, scale, q_ref, k_ref, v_ref, *refs):
    if last:
        _, lse_in_ref, out_ref, lse_ref, wide_ref = refs
    else:
        out_ref, lse_ref, wide_ref = refs
    g = pl.program_id(0)
    sources, _, per_source, width = q_ref.shape
    keys = k_ref.shape[0]
    wide_ref[:, :width] = v_ref[...]
    wide_ref[:, width:] = jnp.ones((keys, width), jnp.bfloat16)
    fold = scale * math.log2(math.e)

    @pl.when(g == 0)
    def _():
        lse_ref[...] = lse_in_ref[...] if last else jnp.zeros_like(lse_ref)

    deep = sources // TILES
    rows = deep * per_source
    shape = (deep, per_source, width)
    lane = lax.broadcasted_iota(jnp.int32, shape, 2)
    index = lax.broadcasted_iota(jnp.int32, shape, 1)
    mine = lane == index + (first + g) * per_source
    for tile in range(TILES):
        here = slice(tile * deep, (tile + 1) * deep)
        q = q_ref[here, 0].reshape(rows, width)
        highest = None
        for start in range(0, keys, KEY_CHUNK):
            scores = lax.dot_general(
                q,
                k_ref[start : start + KEY_CHUNK],
                (((1,), (1,)), ((), ())),
                preferred_element_type=jnp.float32,
            )
            top = jnp.max(scores, axis=1, keepdims=True)
            top = top if highest is None else jnp.maximum(highest, top)
            weights = jnp.exp2((scores - top) * fold).astype(jnp.bfloat16)
            part = jnp.dot(
                weights, wide_ref[start : start + KEY_CHUNK], preferred_element_type=jnp.float32
            )
            both = part if highest is None else both * jnp.exp2((highest - top) * fold) + part
            highest = top
        total = both[:, width:]
        blended = both[:, :width] / total
        lse = (highest * scale + jnp.log(total)).reshape(shape)
        out_ref[here, :per_source, :] = blended.astype(jnp.bfloat16).reshape(shape)
        lse_ref[here] += jnp.sum(jnp.where(mine, lse, 0.0), axis=1)

    if last:
        table = lse_ref[...]
        coarse = table.astype(jnp.bfloat16).astype(jnp.float32)
        rest = jnp.zeros((sources, LSE_ROWS - 2, width), jnp.float32)
        extra = jnp.concatenate([coarse[:, None, :], (table - coarse)[:, None, :], rest], axis=1)
        out_ref[:, per_source:, :] = extra.astype(jnp.bfloat16)


def near_kernel(sources, capacity, heads, width, scale, q_ref, k_ref, v_ref, choices_ref,
                row_pos_ref, col_pos_ref, out_ref, lse_ref, slot_ref):
    groups, tokens = choices_ref.shape[1:]
    allowed = row_pos_ref[...] <= col_pos_ref[...]
    chosen = columns_of(choices_ref)
    for g in range(groups):
        for j, (block, rank) in enumerate(zip(chosen[g], ranks_of(chosen[g], sources))):
            slot_ref[:, 3 * g + j : 3 * g + j + 1] = block * capacity + rank
        keys = k_ref[:, g * width : (g + 1) * width]
        values = v_ref[:, g * width : (g + 1) * width]
        for h in range(heads):
            at = slice((g * heads + h) * width, (g * heads + h + 1) * width)
            scores = lax.dot_general(
                q_ref[:, at], keys, (((1,), (1,)), ((), ())), preferred_element_type=jnp.float32
            )
            scores = jnp.where(allowed, scores * scale, -jnp.inf)
            highest = jnp.max(scores, axis=1, keepdims=True)
            weights = jnp.exp(scores - highest)
            total = jnp.sum(weights, axis=1, keepdims=True)
            blended = jnp.dot(
                weights.astype(jnp.bfloat16), values, preferred_element_type=jnp.float32
            )
            out_ref[:, at] = blended / total
            lse_ref[:, g * heads + h : g * heads + h + 1] = highest + jnp.log(total)


def merge_kernel(capacity, heads, width, place_ref, near_ref, near_lse_ref, slot_ref, back_ref, *refs):
    out_refs, row_ref = refs[:-1], refs[-1]
    tokens = near_ref.shape[0]
    sources = back_ref.shape[0]
    per_source = heads * capacity
    groups = out_refs[0].shape[0]
    lanes = groups * per_source
    row_width = heads * width
    quarter = tokens // len(out_refs)
    extra = back_ref[:, lanes:, :].astype(jnp.float32)
    coarse = extra[:, 0, :].astype(jnp.bfloat16)
    fine = extra[:, 1, :].astype(jnp.bfloat16)
    lane = lax.broadcasted_iota(jnp.int32, (lanes, row_width), 0)
    column = lax.broadcasted_iota(jnp.int32, (lanes, row_width), 1)
    spread = ((lane // capacity) % heads == column // width).astype(jnp.float32)
    spread = spread.astype(jnp.bfloat16)
    block_ids = lax.broadcasted_iota(jnp.int32, (tokens, sources), 1)
    slot_ids = lax.broadcasted_iota(jnp.int32, (tokens, sources * capacity), 1)
    lane_ids = lax.broadcasted_iota(jnp.int32, (tokens, lanes), 1)
    for g in range(groups):
        slots = [slot_ref[:, 3 * g + j : 3 * g + j + 1] for j in range(3)]
        pick = jnp.concatenate([(slot == slot_ids).astype(jnp.float32) for slot in slots], axis=0)
        block = jnp.concatenate(
            [(slot // capacity == block_ids).astype(jnp.float32) for slot in slots], axis=0
        ).astype(jnp.bfloat16)
        in_group = lane_ids // per_source == g
        rank = jnp.concatenate(
            [
                (in_group & (lane_ids % capacity == slot % capacity)).astype(jnp.float32)
                for slot in slots
            ],
            axis=0,
        )
        rows = back_ref[:, g * per_source : (g + 1) * per_source, :].astype(jnp.float32)
        by_head = [
            rows[:, h * capacity : (h + 1) * capacity, :].reshape(sources * capacity, width)
            for h in range(heads)
        ]
        table = jnp.concatenate(by_head, axis=1).astype(jnp.bfloat16)
        got = jnp.dot(pick.astype(jnp.bfloat16), table, preferred_element_type=jnp.float32)
        lse = jnp.zeros((3 * tokens, row_width), jnp.float32)
        for part in (coarse, fine):
            picked = jnp.dot(block, part, preferred_element_type=jnp.float32)
            picked = (picked * rank).astype(jnp.bfloat16)
            lse += jnp.dot(picked, spread, preferred_element_type=jnp.float32)
        near_lse = jnp.concatenate(
            [
                jnp.broadcast_to(near_lse_ref[:, k : k + 1], (tokens, width))
                for k in range(g * heads, (g + 1) * heads)
            ],
            axis=1,
        )
        at = slice(g * row_width, (g + 1) * row_width)
        all_lse = [near_lse] + [lse[j * tokens : (j + 1) * tokens] for j in range(3)]
        all_out = [near_ref[:, at]] + [got[j * tokens : (j + 1) * tokens] for j in range(3)]
        highest = all_lse[0]
        for item in all_lse[1:]:
            highest = jnp.maximum(highest, item)
        top = jnp.zeros((tokens, row_width), jnp.float32)
        bottom = jnp.zeros((tokens, row_width), jnp.float32)
        for item, part in zip(all_lse, all_out):
            weight = jnp.exp(item - highest)
            top += weight * part
            bottom += weight
        row_ref[...] = top / bottom
        for step, out_ref in enumerate(out_refs):
            target = lax.rem(place_ref[0] + step, len(out_refs))
            start = pl.multiple_of(target * quarter, quarter)
            out_ref[g] = row_ref[pl.ds(start, quarter)].astype(jnp.bfloat16)


def assemble_kernel(place_ref, *refs):
    piece_refs, out_ref = refs[:-1], refs[-1]
    count = len(piece_refs)
    for step, piece_ref in enumerate(piece_refs):
        out_ref[lax.rem(place_ref[0] + count - step, count)] = piece_ref[...]


def local(queries, hist_keys, hist_values, own_keys, own_values, choices, positions):
    sources = lax.axis_size("ctx")
    members = lax.axis_size("head")
    tokens, groups, row_width = queries.shape
    keys, _, width = hist_keys.shape
    heads = row_width // width
    capacity = 4 * tokens // sources
    per_source = heads * capacity
    scale = width ** (-0.5)
    quarter = tokens // members
    bf16, f32 = jnp.bfloat16, jnp.float32
    smem = pl.BlockSpec(memory_space=pltpu.SMEM)

    params = pltpu.CompilerParams(vmem_limit_bytes=WIDE_LIMIT)
    small = pltpu.CompilerParams(vmem_limit_bytes=SMALL_LIMIT)

    flat_queries = queries.reshape(tokens, groups * row_width)
    turned = jnp.transpose(choices, (2, 0, 1))

    def dispatch(first, count):
        return pl.pallas_call(
            lambda *refs: dispatch_kernel(first, sources, capacity, heads, width, *refs),
            out_shape=jax.ShapeDtypeStruct((sources, count, per_source, width), bf16),
            in_specs=[whole()] * 2,
            out_specs=whole(),
            compiler_params=small,
            cost_estimate=pl.CostEstimate(
                flops=2 * count * sources * capacity * tokens * row_width,
                transcendentals=0,
                bytes_accessed=2 * (count * sources * capacity + tokens * groups) * row_width,
            ),
            name="dispatch",
        )(flat_queries, turned)

    flat_keys = hist_keys.reshape(keys, groups * width)
    flat_values = hist_values.reshape(keys, groups * width)
    sent = [dispatch(0, SPLIT[0]), dispatch(SPLIT[0], SPLIT[1])]
    sent[1], flat_keys, flat_values = lax.optimization_barrier((sent[1], flat_keys, flat_values))
    received = [lax.all_to_all(item, "ctx", 0, 0, tiled=True) for item in sent]

    def far(part, *before):
        last = part == 1
        first = SPLIT[0] if last else 0
        out_rows = groups * per_source + LSE_ROWS
        work = SPLIT[part] * sources * per_source * keys
        extra_specs = [
            pl.BlockSpec(memory_space=pl.ANY),
            pl.BlockSpec((sources, groups * per_source), lambda g: (0, 0)),
        ]
        if last:
            tail = pl.Element(per_source + LSE_ROWS)
            block = (pl.Element(sources), tail, pl.Element(width))
            out_spec = pl.BlockSpec(block, lambda g: (0, first * per_source, 0))
        else:
            out_spec = pl.BlockSpec((sources, per_source, width), lambda g: (0, g, 0))
        return pl.pallas_call(
            lambda *refs: far_kernel(first, last, scale, *refs),
            grid=(SPLIT[part],),
            in_specs=[
                pl.BlockSpec((sources, 1, per_source, width), lambda g: (0, g, 0, 0)),
                pl.BlockSpec((keys, width), lambda g: (0, first + g)),
                pl.BlockSpec((keys, width), lambda g: (0, first + g)),
            ]
            + (extra_specs if last else []),
            out_specs=[
                out_spec,
                pl.BlockSpec((sources, groups * per_source), lambda g: (0, 0)),
            ],
            out_shape=[
                jax.ShapeDtypeStruct((sources, out_rows, width), bf16),
                jax.ShapeDtypeStruct((sources, groups * per_source), f32),
            ],
            scratch_shapes=[pltpu.VMEM((keys, 2 * width), bf16)],
            input_output_aliases={3: 0} if last else {},
            compiler_params=params,
            cost_estimate=pl.CostEstimate(
                flops=6 * work * width, transcendentals=work, bytes_accessed=4 * work // keys * width
            ),
            name="far",
        )(received[part], flat_keys, flat_values, *before)

    parts, _ = far(1, *far(0))
    back = lax.all_to_all(parts, "ctx", 0, 0, tiled=True)

    near = pl.pallas_call(
        lambda *refs: near_kernel(sources, capacity, heads, width, scale, *refs),
        out_shape=[
            jax.ShapeDtypeStruct((tokens, groups * row_width), f32),
            jax.ShapeDtypeStruct((tokens, width), f32),
            jax.ShapeDtypeStruct((tokens, width), jnp.int32),
        ],
        in_specs=[whole()] * 6,
        out_specs=[whole()] * 3,
        compiler_params=params,
        cost_estimate=pl.CostEstimate(
            flops=4 * tokens * tokens * groups * row_width,
            transcendentals=tokens * tokens * groups * heads,
            bytes_accessed=16 * tokens * groups * row_width,
        ),
        name="near",
    )(
        flat_queries,
        own_keys.reshape(tokens, groups * width),
        own_values.reshape(tokens, groups * width),
        turned,
        positions,
        positions.reshape(tokens, 1),
    )

    place = lax.axis_index("head").astype(jnp.int32).reshape(1)
    made = pl.pallas_call(
        lambda *refs: merge_kernel(capacity, heads, width, *refs),
        out_shape=[jax.ShapeDtypeStruct((groups, quarter, row_width), bf16)] * members,
        in_specs=[smem] + [whole()] * 4,
        out_specs=[whole()] * members,
        scratch_shapes=[pltpu.VMEM((tokens, row_width), f32)],
        compiler_params=small,
        name="merge",
    )(place, *near, back)
    pieces = []
    for step, item in enumerate(made):
        pairs = [(i, (i + step) % members) for i in range(members)]
        pieces.append(lax.ppermute(item, "head", pairs) if step else item)
    joined = pl.pallas_call(
        assemble_kernel,
        out_shape=jax.ShapeDtypeStruct((members, groups, quarter, row_width), bf16),
        in_specs=[smem] + [whole()] * len(pieces),
        out_specs=whole(),
        compiler_params=small,
        name="assemble",
    )(place, *pieces)
    joined = joined.reshape(members * groups, quarter, row_width)
    return jnp.transpose(joined, (1, 0, 2))


def solution(mesh):
    in_specs = (
        P("ctx", "head", None),
        P("ctx", "head", None),
        P("ctx", "head", None),
        P("ctx", "head", None),
        P("ctx", "head", None),
        P("head", "ctx", None),
        P("ctx", None),
    )
    out_specs = P(("ctx", "head"), None, None)
    return jax.shard_map(local, mesh=mesh, in_specs=in_specs, out_specs=out_specs, check_vma=False)
```

time: 181 us -> 175 us (0.967)
  blocking collectives: 55.1 us -> 0 us
  waiting for transfers between devices: 38.5 us -> 85 us
  starting transfers between devices: 18.6 us -> 35.2 us
  Pallas kernels: 55.4 us -> 41.3 us
    all_to_all x2 -> x0, blocking collectives: 55.1 us -> none  [the longest x1 41.8 us: local(): lax.all_to_all(item, 'ctx', 0, 0, tiled=True)]
    all_to_all x3, waiting for transfers between devices: 38.5 us -> 80 us  [the longest x1 46.7 us: local(): back = lax.all_to_all(parts, 'ctx', 0, 0, tiled=True)]
    all_to_all x3, starting transfers between devices: 18.6 us -> 30.1 us  [the longest x2 19.4 us: local(): received = [lax.all_to_all(item, 'ctx', 0, 0, tiled=True) for item in sent]]
    pallas_call x3 -> x5, Pallas kernels: 41.9 us -> 32.3 us  [the longest x2 27.3 us: far(): pl.pallas_call(lambda *refs: far_kernel(first, last, scale, *refs), grid=...]
    ppermute x0 -> x3, starting transfers between devices: none -> 5.05 us  [local(): pieces.append(lax.ppermute(item, 'head', pairs) if step else item)]
    ppermute x0 -> x3, waiting for transfers between devices: none -> 4.99 us  [local(): pieces.append(lax.ppermute(item, 'head', pairs) if step else item)]
    pallas_call x1, Pallas kernels: 6.71 us -> 3.31 us  [local(): pl.pallas_call(lambda *refs: merge_kernel(capacity, heads, width, *refs),...]
    unnamed x16 -> x23, local copies, waits for them, and re-layouts: 4.56 us -> 5.58 us
  transfers between devices with their start and end apart: 3 -> 6, of which waited for: 3 -> 4; matrix products, arithmetic and copies ran while one was open for 3% -> 3% of each run, Pallas kernels for 24% -> 15%
where the time goes in v2:
time: 175 us; the launch traced here: 174 us
  waiting for transfers between devices  85 us (49%)
  Pallas kernels  41.3 us (24%)
  starting transfers between devices  35.2 us (20%)
  local copies, waits for them, and re-layouts  12.7 us (7%)
    all_to_all x1, waiting for transfers between devices, local(): back = lax.all_to_all(parts, 'ctx', 0, 0, tiled=True)  46.7 us
    all_to_all x2, waiting for transfers between devices, local(): received = [lax.all_to_all(item, 'ctx', 0, 0, tiled=True) for item in sent]  33.3 us
    pallas_call x2, Pallas kernels, far(): pl.pallas_call(lambda *refs: far_kernel(first, last, scale, *refs), grid=...  27.3 us
    all_to_all x2, starting transfers between devices, local(): received = [lax.all_to_all(item, 'ctx', 0, 0, tiled=True) for item in sent]  19.4 us
    all_to_all x1, starting transfers between devices, local(): back = lax.all_to_all(parts, 'ctx', 0, 0, tiled=True)  10.7 us
    pallas_call x1, Pallas kernels, local(): pl.pallas_call(lambda *refs: near_kernel(sources, capacity, heads, width,...  5.66 us
    unnamed x23, local copies, waits for them, and re-layouts  5.58 us
    ppermute x3, starting transfers between devices, local(): pieces.append(lax.ppermute(item, 'head', pairs) if step else item)  5.05 us
  transfers between devices with their start and end apart: 6, of which 4 were waited for; matrix products, arithmetic and copies ran while one was open for 3% of the time, Pallas kernels for 15%

profile of v2, /device:TPU:1, one launch (start us, length us, event | category | flops | bytes accessed | tf_op | source)
XLA Modules:
  0.0 174.3 jit_solution(11358135379341939524)
XLA Ops:
  0.0 1.1 copy.11
  1.1 0.0 copy-start
  1.2 0.0 copy-start.4
  1.2 0.7 copy-done.4
  1.9 3.2 %dispatch.3 = bf16[64,3,32,128]{3,2,1,0:T(8,128)(2,1)} custom-call(bf16[128,2048]{1,0:T(8,128)(2,1)S(1)} %bitcast.21, s32[3,4,128]{2,1,0:T(4,128)S(1)} %bitcast.26), custom_call_target="tpu_custom_call" | custom-call | flops 201326592 | bytes 2097152 | tf_op jit(solution)/shard_map/dispatch/pallas_call | solution.py:240
  5.1 0.0 copy-start.5
  5.1 0.0 copy-start.6
  5.1 13.3 %all-to-all-start.1 = ((bf16[64,3,32,128]{3,2,1,0:T(8,128)(2,1)}), bf16[64,3,32,128]{3,2,1,0:T(8,128)(2,1)}, u32[]{:S(2)}, u32[]{:S(2)}) async-start(bf16[64,3,32,128]{3,2,1,0:T(8,128)(2,1)} %dispatch.3), calls=%async_computation.1 | async-start | bytes 3145728 | tf_op jit(solution)/shard_map/all_to_all | solution.py:258
  18.4 0.0 copy-done
  18.4 0.0 copy-done.5
  18.4 1.8 %dispatch.2 = bf16[64,1,32,128]{3,2,1,0:T(8,128)(2,1)} custom-call(bf16[128,2048]{1,0:T(8,128)(2,1)S(1)} %bitcast.22, s32[3,4,128]{2,1,0:T(4,128)S(1)} %bitcast.27), custom_call_target="tpu_custom_call" | custom-call | flops 67108864 | bytes 1048576 | tf_op jit(solution)/shard_map/dispatch/pallas_call | solution.py:240
  20.1 0.0 copy-done.6
  20.1 4.6 %copy_bitcast_fusion = (bf16[2048,512]{1,0:T(8,128)(2,1)}, bf16[2048,512]{1,0:T(8,128)(2,1)}) fusion(bf16[256,8,4,128]{3,2,1,0:T(4,128)(2,1)S(1)} %bitcast.28, bf16[256,8,4,128]{3,2,1,0:T(4,128)(2,1)} %bitcast.29), kind=kLoop, calls=%fused_computation | loop fusion | bytes 8388608 | tf_op jit(solution)/shard_map/reshape | solution.py:255
  24.8 33.3 %all-to-all-done.1.refs_0_ = bf16[64,3,32,128]{3,2,1,0:T(8,128)(2,1)} async-done(((bf16[64,3,32,128]{3,2,1,0:T(8,128)(2,1)}), bf16[64,3,32,128]{3,2,1,0:T(8,128)(2,1)}, u32[]{:S(2)}, u32[]{:S(2)}) %all-to-all-start.1) | async-done | bytes 1572896 | tf_op jit(solution)/shard_map/all_to_all | solution.py:258
  58.1 6.1 %all-to-all-start = ((bf16[64,1,32,128]{3,2,1,0:T(8,128)(2,1)}), bf16[64,1,32,128]{3,2,1,0:T(8,128)(2,1)S(1)}, u32[]{:S(2)}, u32[]{:S(2)}) async-start(bf16[64,1,32,128]{3,2,1,0:T(8,128)(2,1)} %dispatch.2), calls=%async_computation | async-start | bytes 1048576 | tf_op jit(solution)/shard_map/all_to_all | solution.py:258
  64.2 19.2 %far.2 = (bf16[64,136,128]{2,1,0:T(8,128)(2,1)}, f32[64,128]{1,0:T(8,128)}) custom-call(bf16[64,3,32,128]{3,2,1,0:T(8,128)(2,1)} %all-to-all-done.1.refs_0_, bf16[2048,512]{1,0:T(8,128)(2,1)} %get-tuple-element.22.refs_1_, bf16[2048,512]{1,0:T(8,128)(2,1)} %get-tuple-element.23.refs_2_), custom_call_target="tpu_custom_call" | custom-call | flops 9663676416 | bytes 3145728 | tf_op jit(solution)/shard_map/far/pallas_call | solution.py:275
  83.4 0.0 all-to-all-done.refs_0_
  83.4 0.0 copy-start.7
  83.5 0.8 copy-done.7
  84.3 8.1 %far.3 = (bf16[64,136,128]{2,1,0:T(8,128)(2,1)}, f32[64,128]{1,0:T(8,128)}) custom-call(bf16[64,1,32,128]{3,2,1,0:T(8,128)(2,1)} %copy-done.7, bf16[2048,512]{1,0:T(8,128)(2,1)} %get-tuple-element.22.refs_1_, bf16[2048,512]{1,0:T(8,128)(2,1)} %get-tuple-element.23.refs_2_, ...), custom_call_target="tpu_custom_call", output_to_operand_aliasing={{0}: (3, {})} | custom-call | flops 3221225472 | bytes 1048576 | tf_op jit(solution)/shard_map/far/pallas_call | solution.py:275
  92.4 0.0 copy-start.10
  92.4 0.0 copy-start.8
  92.4 0.0 copy-start.9
  92.4 10.7 %all-to-all-start.2 = ((bf16[64,136,128]{2,1,0:T(8,128)(2,1)}), bf16[64,136,128]{2,1,0:T(8,128)(2,1)S(1)}, u32[]{:S(2)}, u32[]{:S(2)}) async-start(bf16[64,136,128]{2,1,0:T(8,128)(2,1)} %get-tuple-element.26), calls=%async_computation.2 | async-start | bytes 4456448 | tf_op jit(solution)/shard_map/all_to_all | solution.py:302
  103.1 0.0 copy-done.10
  103.1 0.7 copy.9.refs_5_
  103.8 0.0 copy-done.8
  103.8 0.0 copy-done.9
  103.8 0.7 copy_bitcast_fusion.3
  104.5 5.7 %near.1 = (f32[128,2048]{1,0:T(8,128)}, f32[128,128]{1,0:T(8,128)}, s32[128,128]{1,0:T(8,128)}) custom-call(bf16[128,2048]{1,0:T(8,128)(2,1)} %bitcast.23, bf16[128,512]{1,0:T(8,128)(2,1)} %get-tuple-element.32.refs_1_, bf16[128,512]{1,0:T(8,128)(2,1)} %get-tuple-element.31.refs_2_, s32[3,4,128]{2,1,0:T(4,128)} %bitcast.25, s32[1,128]{1,0:T(1,128)} %refs_4_.1, ...), custom_call_target="tpu_custom_call" | custom-call | flops 134217728 | bytes 4194304 | tf_op jit(solution)/shard_map/near/pallas_call | solution.py:304
  110.2 46.7 %all-to-all-done.2.refs_4_ = bf16[64,136,128]{2,1,0:T(8,128)(2,1)S(1)} async-done(((bf16[64,136,128]{2,1,0:T(8,128)(2,1)}), bf16[64,136,128]{2,1,0:T(8,128)(2,1)S(1)}, u32[]{:S(2)}, u32[]{:S(2)}) %all-to-all-start.2) | async-done | bytes 2228256 | tf_op jit(solution)/shard_map/all_to_all | solution.py:302
  156.9 0.0 copy-start.1
  156.9 1.2 copy-done.1
  158.1 0.0 copy-start.2
  158.1 0.8 copy-done.2
  159.0 0.0 copy-start.3
  159.0 0.8 copy-done.3
  159.8 3.3 %merge.1 = (bf16[4,32,512]{2,1,0:T(8,128)(2,1)S(1)}, bf16[4,32,512]{2,1,0:T(8,128)(2,1)S(1)}, bf16[4,32,512]{2,1,0:T(8,128)(2,1)S(1)}, bf16[4,32,512]{2,1,0:T(8,128)(2,1)S(1)}) custom-call(s32[1]{0:T(128)} %bitcast.refs_0_.place_ref, f32[128,2048]{1,0:T(8,128)S(1)} %copy-done.1, f32[128,128]{1,0:T(8,128)S(1)} %copy-done.2, s32[128,128]{1,0:T(8,128)S(1)} %copy-done.3, ...), custom_call_target="tpu_custom_call" | custom-call | tf_op jit(solution)/shard_map/merge/pallas_call | solution.py:330
  163.1 1.4 collective-permute-start
  164.5 2.6 %collective-permute-start.1 = (bf16[4,32,512]{2,1,0:T(8,128)(2,1)S(1)}, bf16[4,32,512]{2,1,0:T(8,128)(2,1)S(1)}, u32[]{:S(2)}, u32[]{:S(2)}) collective-permute-start(bf16[4,32,512]{2,1,0:T(8,128)(2,1)S(1)} %get-tuple-element.29), channel_id=1, source_target_pairs={{0,2},{1,3},{2,0},{3,1},{4,6},{5,7},{6,4},{7,5},{8,10},{9,11},{10,... | collective-permute-start | bytes 393224 | tf_op jit(solution)/shard_map/ppermute | solution.py:342
  167.1 1.1 collective-permute-start.2
  168.2 1.1 collective-permute-done.refs_1_
  169.3 3.9 %collective-permute-done.1.refs_2_ = bf16[4,32,512]{2,1,0:T(8,128)(2,1)S(1)} collective-permute-done((bf16[4,32,512]{2,1,0:T(8,128)(2,1)S(1)}, bf16[4,32,512]{2,1,0:T(8,128)(2,1)S(1)}, u32[]{:S(2)}, u32[]{:S(2)}) %collective-permute-start.1) | collective-permute-done | bytes 131104 | tf_op jit(solution)/shard_map/ppermute | solution.py:342
  173.2 0.0 collective-permute-done.2.refs_3_
  173.2 1.1 copy.21
  (1 shorter events, 0.0 us)
Async XLA Ops:
  1.1 17.2 %copy-start = (bf16[16,8,4,512]{3,1,2,0:T(8,128)(2,1)}, bf16[16,8,4,512]{3,1,2,0:T(8,128)(2,1)S(1)}, u32[]{:S(2)}) copy-start(bf16[16,8,4,512]{3,1,2,0:T(8,128)(2,1)S(1)} %copy.11) | copy-start | bytes 1572868
  1.2 0.7 copy-start.4
  5.1 13.3 %copy-start.5 = (s32[4,128,3]{1,0,2:T(4,128)S(1)}, s32[4,128,3]{1,0,2:T(4,128)}, u32[]{:S(2)}) copy-start(s32[4,128,3]{1,0,2:T(4,128)} %param.12) | copy-start | bytes 18436
  5.1 15.1 %copy-start.6 = (bf16[2048,4,128]{2,1,0:T(4,128)(2,1)S(1)}, bf16[2048,4,128]{2,1,0:T(4,128)(2,1)}, u32[]{:S(2)}) copy-start(bf16[2048,4,128]{2,1,0:T(4,128)(2,1)} %param.9) | copy-start | bytes 6291460
  5.1 53.0 %all-to-all-start.1 = ((bf16[64,3,32,128]{3,2,1,0:T(8,128)(2,1)}), bf16[64,3,32,128]{3,2,1,0:T(8,128)(2,1)}, u32[]{:S(2)}, u32[]{:S(2)}) async-start(bf16[64,3,32,128]{3,2,1,0:T(8,128)(2,1)} %dispatch.3), calls=%async_computation.1 | async-start | bytes 3145728 | tf_op jit(solution)/shard_map/all_to_all | solution.py:258
  58.1 25.4 %all-to-all-start = ((bf16[64,1,32,128]{3,2,1,0:T(8,128)(2,1)}), bf16[64,1,32,128]{3,2,1,0:T(8,128)(2,1)S(1)}, u32[]{:S(2)}, u32[]{:S(2)}) async-start(bf16[64,1,32,128]{3,2,1,0:T(8,128)(2,1)} %dispatch.2), calls=%async_computation | async-start | bytes 1048576 | tf_op jit(solution)/shard_map/all_to_all | solution.py:258
  83.4 0.8 copy-start.7
  92.4 10.7 %copy-start.10 = (s32[1,128]{1,0:T(1,128)S(1)}, s32[1,128]{1,0:T(1,128)}, u32[]{:S(2)}) copy-start(s32[1,128]{1,0:T(1,128)} %refs_4_.1) | copy-start | bytes 1540
  92.4 11.4 %copy-start.8 = (bf16[128,4,128]{2,1,0:T(4,128)(2,1)S(1)}, bf16[128,4,128]{2,1,0:T(4,128)(2,1)}, u32[]{:S(2)}) copy-start(bf16[128,4,128]{2,1,0:T(4,128)(2,1)} %param.11) | copy-start | bytes 393220
  92.4 11.4 %copy-start.9 = (bf16[128,4,128]{2,1,0:T(4,128)(2,1)S(1)}, bf16[128,4,128]{2,1,0:T(4,128)(2,1)}, u32[]{:S(2)}) copy-start(bf16[128,4,128]{2,1,0:T(4,128)(2,1)} %param.10) | copy-start | bytes 393220
  92.4 64.5 %all-to-all-start.2 = ((bf16[64,136,128]{2,1,0:T(8,128)(2,1)}), bf16[64,136,128]{2,1,0:T(8,128)(2,1)S(1)}, u32[]{:S(2)}, u32[]{:S(2)}) async-start(bf16[64,136,128]{2,1,0:T(8,128)(2,1)} %get-tuple-element.26), calls=%async_computation.2 | async-start | bytes 4456448 | tf_op jit(solution)/shard_map/all_to_all | solution.py:302
  156.9 1.2 copy-start.1
  158.1 0.8 copy-start.2
  159.0 0.8 copy-start.3
  163.1 6.1 %collective-permute-start = (bf16[4,32,512]{2,1,0:T(8,128)(2,1)S(1)}, bf16[4,32,512]{2,1,0:T(8,128)(2,1)S(1)}, u32[]{:S(2)}, u32[]{:S(2)}) collective-permute-start(bf16[4,32,512]{2,1,0:T(8,128)(2,1)S(1)} %get-tuple-element.28), channel_id=1, source_target_pairs={{0,1},{1,2},{2,3},{3,0},{4,5},{5,6},{6,7},{7,4},{8,9},{9,10},{10,1... | collective-permute-start | bytes 393224 | tf_op jit(solution)/shard_map/ppermute | solution.py:342
  164.5 8.7 %collective-permute-start.1 = (bf16[4,32,512]{2,1,0:T(8,128)(2,1)S(1)}, bf16[4,32,512]{2,1,0:T(8,128)(2,1)S(1)}, u32[]{:S(2)}, u32[]{:S(2)}) collective-permute-start(bf16[4,32,512]{2,1,0:T(8,128)(2,1)S(1)} %get-tuple-element.29), channel_id=1, source_target_pairs={{0,2},{1,3},{2,0},{3,1},{4,6},{5,7},{6,4},{7,5},{8,10},{9,11},{10,... | collective-permute-start | bytes 393224 | tf_op jit(solution)/shard_map/ppermute | solution.py:342
  167.1 6.1 %collective-permute-start.2 = (bf16[4,32,512]{2,1,0:T(8,128)(2,1)S(1)}, bf16[4,32,512]{2,1,0:T(8,128)(2,1)S(1)}, u32[]{:S(2)}, u32[]{:S(2)}) collective-permute-start(bf16[4,32,512]{2,1,0:T(8,128)(2,1)S(1)} %get-tuple-element.30), channel_id=1, source_target_pairs={{0,3},{1,0},{2,1},{3,2},{4,7},{5,4},{6,5},{7,6},{8,11},{9,8},{10,9... | collective-permute-start | bytes 393224 | tf_op jit(solution)/shard_map/ppermute | solution.py:342

commit v3 on v2

v3 whole, which is shorter than its diff:
```python
import math

import jax
import jax.numpy as jnp
from jax import lax
from jax.experimental import pallas as pl
from jax.experimental.pallas import tpu as pltpu
from jax.sharding import PartitionSpec as P

PARTS = ((0, 2), (2, 2))
LSE_ROWS = 8
KEY_CHUNK = 256
TILES = 4
ORDER = (2, 1, 3)
WIDE_LIMIT = 60 * 1024 * 1024
SMALL_LIMIT = 24 * 1024 * 1024


def whole():
    return pl.BlockSpec(memory_space=pltpu.VMEM)


def columns_of(choices_ref):
    count, groups, tokens = choices_ref.shape
    rows = choices_ref[...].astype(jnp.float32).reshape(count * groups, tokens)
    pad = jnp.zeros((tokens - count * groups, tokens), jnp.float32)
    columns = jnp.concatenate([rows, pad], axis=0).T.astype(jnp.int32)
    return [[columns[:, j * groups + g : j * groups + g + 1] for j in range(count)] for g in range(groups)]


def ranks_of(chosen, sources):
    tokens = chosen[0].shape[0]
    block_ids = lax.broadcasted_iota(jnp.int32, (tokens, sources), 1)
    hits = [(item == block_ids).astype(jnp.float32) for item in chosen]
    occupied = (hits[0] + hits[1] + hits[2]).astype(jnp.bfloat16)
    row = lax.broadcasted_iota(jnp.int32, (tokens, tokens), 0)
    column = lax.broadcasted_iota(jnp.int32, (tokens, tokens), 1)
    before = (column < row).astype(jnp.bfloat16)
    earlier = jnp.dot(before, occupied, preferred_element_type=jnp.float32)
    return [jnp.sum(hit * earlier, axis=1, keepdims=True).astype(jnp.int32) for hit in hits]


def fill_slots(picked, rows, sources, capacity, heads, width):
    pick = picked.astype(jnp.float32).T.astype(jnp.bfloat16)
    filled = jnp.dot(pick, rows, preferred_element_type=jnp.float32)
    filled = filled.reshape(sources, capacity, heads * width)
    by_head = [filled[:, :, h * width : (h + 1) * width] for h in range(heads)]
    return jnp.concatenate(by_head, axis=1).astype(jnp.bfloat16)


def dispatch_kernel(first, sources, capacity, heads, width, q_ref, choices_ref, out_ref):
    tokens = choices_ref.shape[2]
    row_width = heads * width
    chosen = columns_of(choices_ref)
    slot_ids = lax.broadcasted_iota(jnp.int32, (tokens, sources * capacity), 1)
    for i in range(out_ref.shape[1]):
        g = first + i
        hit = None
        for block, rank in zip(chosen[g], ranks_of(chosen[g], sources)):
            mine = block * capacity + rank == slot_ids
            hit = mine if hit is None else hit | mine
        rows = q_ref[:, g * row_width : (g + 1) * row_width]
        out_ref[:, i] = fill_slots(hit, rows, sources, capacity, heads, width)


def far_group(scale, slot, q_ref, k_ref, v_ref, out_ref, lse_ref, wide_ref):
    sources, _, per_source, width = q_ref.shape
    keys = k_ref.shape[0]
    wide_ref[:, :width] = v_ref[...]
    wide_ref[:, width:] = jnp.ones((keys, width), jnp.bfloat16)
    fold = scale * math.log2(math.e)
    deep = sources // TILES
    rows = deep * per_source
    shape = (deep, per_source, width)
    lane = lax.broadcasted_iota(jnp.int32, shape, 2)
    index = lax.broadcasted_iota(jnp.int32, shape, 1)
    mine = lane == index + slot * per_source
    for tile in range(TILES):
        here = slice(tile * deep, (tile + 1) * deep)
        q = q_ref[here, 0].reshape(rows, width)
        highest = None
        for start in range(0, keys, KEY_CHUNK):
            scores = lax.dot_general(
                q,
                k_ref[start : start + KEY_CHUNK],
                (((1,), (1,)), ((), ())),
                preferred_element_type=jnp.float32,
            )
            top = jnp.max(scores, axis=1, keepdims=True)
            top = top if highest is None else jnp.maximum(highest, top)
            weights = jnp.exp2((scores - top) * fold).astype(jnp.bfloat16)
            part = jnp.dot(
                weights, wide_ref[start : start + KEY_CHUNK], preferred_element_type=jnp.float32
            )
            both = part if highest is None else both * jnp.exp2((highest - top) * fold) + part
            highest = top
        total = both[:, width:]
        blended = both[:, :width] / total
        lse = (highest * scale + jnp.log(total)).reshape(shape)
        out_ref[here] = blended.astype(jnp.bfloat16).reshape(shape)
        lse_ref[here] += jnp.sum(jnp.where(mine, lse, 0.0), axis=1)


def far_kernel(scale, groups, q_ref, k_ref, v_ref, out_ref, lse_ref, wide_ref):
    g = pl.program_id(0)
    sources, width = q_ref.shape[0], k_ref.shape[1]

    @pl.when(g == 0)
    def _():
        lse_ref[...] = jnp.zeros_like(lse_ref)

    @pl.when(g < groups)
    def _():
        far_group(scale, g, q_ref, k_ref, v_ref, out_ref, lse_ref, wide_ref)

    @pl.when(g == groups)
    def _():
        table = lse_ref[...]
        coarse = table.astype(jnp.bfloat16).astype(jnp.float32)
        rest = jnp.zeros((sources, out_ref.shape[1] - 2, width), jnp.float32)
        extra = jnp.concatenate([coarse[:, None, :], (table - coarse)[:, None, :], rest], axis=1)
        out_ref[...] = extra.astype(jnp.bfloat16)


def near_kernel(sources, capacity, heads, width, scale, q_ref, k_ref, v_ref, choices_ref,
                row_pos_ref, col_pos_ref, out_ref):
    groups, tokens = choices_ref.shape[1:]
    allowed = row_pos_ref[...] <= col_pos_ref[...]
    chosen = columns_of(choices_ref)
    for g in range(groups):
        for j, (block, rank) in enumerate(zip(chosen[g], ranks_of(chosen[g], sources))):
            column = (groups * heads + 1) * width + 3 * g + j
            out_ref[:, column : column + 1] = (block * capacity + rank).astype(jnp.float32)
        keys = k_ref[:, g * width : (g + 1) * width]
        values = v_ref[:, g * width : (g + 1) * width]
        for h in range(heads):
            at = slice((g * heads + h) * width, (g * heads + h + 1) * width)
            scores = lax.dot_general(
                q_ref[:, at], keys, (((1,), (1,)), ((), ())), preferred_element_type=jnp.float32
            )
            scores = jnp.where(allowed, scores * scale, -jnp.inf)
            highest = jnp.max(scores, axis=1, keepdims=True)
            weights = jnp.exp(scores - highest)
            total = jnp.sum(weights, axis=1, keepdims=True)
            blended = jnp.dot(
                weights.astype(jnp.bfloat16), values, preferred_element_type=jnp.float32
            )
            out_ref[:, at] = blended / total
            column = groups * heads * width + g * heads + h
            out_ref[:, column : column + 1] = highest + jnp.log(total)


def merge_kernel(first, groups, capacity, heads, width, place_ref, near_ref, back_ref, *refs):
    out_refs, row_ref = refs[:-1], refs[-1]
    tokens = near_ref.shape[0]
    sources = back_ref.shape[0]
    per_source = heads * capacity
    count = out_refs[0].shape[0]
    lanes = back_ref.shape[2]
    row_width = heads * width
    quarter = tokens // len(out_refs)
    extra = back_ref[:, count * per_source :, :].astype(jnp.float32)
    coarse = extra[:, 0, :].astype(jnp.bfloat16)
    fine = extra[:, 1, :].astype(jnp.bfloat16)
    lane = lax.broadcasted_iota(jnp.int32, (lanes, row_width), 0)
    column = lax.broadcasted_iota(jnp.int32, (lanes, row_width), 1)
    spread = ((lane // capacity) % heads == column // width).astype(jnp.float32)
    spread = spread.astype(jnp.bfloat16)
    block_ids = lax.broadcasted_iota(jnp.int32, (tokens, sources), 1)
    slot_ids = lax.broadcasted_iota(jnp.int32, (tokens, sources * capacity), 1)
    lane_ids = lax.broadcasted_iota(jnp.int32, (tokens, lanes), 1)
    for i in range(count):
        g = first + i
        slot_at = (groups * heads + 1) * width + 3 * g
        slots = [near_ref[:, slot_at + j : slot_at + j + 1].astype(jnp.int32) for j in range(3)]
        pick = jnp.concatenate([(slot == slot_ids).astype(jnp.float32) for slot in slots], axis=0)
        block = jnp.concatenate(
            [(slot // capacity == block_ids).astype(jnp.float32) for slot in slots], axis=0
        ).astype(jnp.bfloat16)
        in_group = lane_ids // per_source == i
        rank = jnp.concatenate(
            [
                (in_group & (lane_ids % capacity == slot % capacity)).astype(jnp.float32)
                for slot in slots
            ],
            axis=0,
        )
        rows = back_ref[:, i * per_source : (i + 1) * per_source, :].astype(jnp.float32)
        by_head = [
            rows[:, h * capacity : (h + 1) * capacity, :].reshape(sources * capacity, width)
            for h in range(heads)
        ]
        table = jnp.concatenate(by_head, axis=1).astype(jnp.bfloat16)
        got = jnp.dot(pick.astype(jnp.bfloat16), table, preferred_element_type=jnp.float32)
        lse = jnp.zeros((3 * tokens, row_width), jnp.float32)
        for part in (coarse, fine):
            picked = jnp.dot(block, part, preferred_element_type=jnp.float32)
            picked = (picked * rank).astype(jnp.bfloat16)
            lse += jnp.dot(picked, spread, preferred_element_type=jnp.float32)
        near_lse = jnp.concatenate(
            [
                jnp.broadcast_to(near_ref[:, k : k + 1], (tokens, width))
                for k in range((groups * width + g) * heads, (groups * width + g + 1) * heads)
            ],
            axis=1,
        )
        at = slice(g * row_width, (g + 1) * row_width)
        all_lse = [near_lse] + [lse[j * tokens : (j + 1) * tokens] for j in range(3)]
        all_out = [near_ref[:, at]] + [got[j * tokens : (j + 1) * tokens] for j in range(3)]
        highest = all_lse[0]
        for item in all_lse[1:]:
            highest = jnp.maximum(highest, item)
        top = jnp.zeros((tokens, row_width), jnp.float32)
        bottom = jnp.zeros((tokens, row_width), jnp.float32)
        for item, part in zip(all_lse, all_out):
            weight = jnp.exp(item - highest)
            top += weight * part
            bottom += weight
        row_ref[...] = top / bottom
        for step, out_ref in enumerate(out_refs):
            target = lax.rem(place_ref[0] + step, len(out_refs))
            start = pl.multiple_of(target * quarter, quarter)
            out_ref[i] = row_ref[pl.ds(start, quarter)].astype(jnp.bfloat16)


def assemble_kernel(count, place_ref, *refs):
    piece_refs, out_ref = refs[:-1], refs[-1]
    for i, piece_ref in enumerate(piece_refs):
        origin = lax.rem(place_ref[0] + count - i % count, count)
        first = PARTS[i // count][0]
        out_ref[origin, first : first + piece_ref.shape[0]] = piece_ref[...]


def local(queries, hist_keys, hist_values, own_keys, own_values, choices, positions):
    sources = lax.axis_size("ctx")
    members = lax.axis_size("head")
    tokens, groups, row_width = queries.shape
    keys, _, width = hist_keys.shape
    heads = row_width // width
    capacity = 4 * tokens // sources
    per_source = heads * capacity
    scale = width ** (-0.5)
    quarter = tokens // members
    bf16, f32 = jnp.bfloat16, jnp.float32
    smem = pl.BlockSpec(memory_space=pltpu.SMEM)

    params = pltpu.CompilerParams(vmem_limit_bytes=WIDE_LIMIT)
    small = pltpu.CompilerParams(vmem_limit_bytes=SMALL_LIMIT)

    flat_queries = queries.reshape(tokens, groups * row_width)
    turned = jnp.transpose(choices, (2, 0, 1))

    group = per_source, width
    work = sources * per_source * keys

    def dispatch(first, count):
        return pl.pallas_call(
            lambda *refs: dispatch_kernel(first, sources, capacity, heads, width, *refs),
            out_shape=jax.ShapeDtypeStruct((sources, count) + group, bf16),
            in_specs=[whole()] * 2,
            out_specs=whole(),
            compiler_params=small,
            name="dispatch",
        )(flat_queries, turned)

    sent = [dispatch(*part) for part in PARTS]
    sent[1], hist_keys, hist_values = lax.optimization_barrier((sent[1], hist_keys, hist_values))
    flat_keys = hist_keys.reshape(keys, groups * width)
    flat_values = hist_values.reshape(keys, groups * width)

    def far(received, first, count):
        def held(g):
            return jnp.minimum(g, count - 1)

        block = pl.BlockSpec((keys, width), lambda g: (0, first + held(g)))
        out_rows = count * per_source + LSE_ROWS
        return pl.pallas_call(
            lambda *refs: far_kernel(scale, count, *refs),
            grid=(count + 1,),
            in_specs=[
                pl.BlockSpec((sources, 1) + group, lambda g: (0, held(g), 0, 0)),
                block,
                block,
            ],
            out_specs=pl.BlockSpec((sources,) + group, lambda g: (0, g, 0)),
            out_shape=jax.ShapeDtypeStruct((sources, out_rows, width), bf16),
            scratch_shapes=[
                pltpu.VMEM((sources, width), f32),
                pltpu.VMEM((keys, 2 * width), bf16),
            ],
            compiler_params=params,
            cost_estimate=pl.CostEstimate(
                flops=6 * count * work * width,
                transcendentals=count * work,
                bytes_accessed=4 * keys * count * width,
            ),
            name="far",
        )(received, flat_keys, flat_values)

    received = [lax.all_to_all(item, "ctx", 0, 0, tiled=True) for item in sent]
    parts = [far(item, *part) for item, part in zip(received, PARTS)]
    back = [lax.all_to_all(item, "ctx", 0, 0, tiled=True) for item in parts]

    near = pl.pallas_call(
        lambda *refs: near_kernel(sources, capacity, heads, width, scale, *refs),
        out_shape=jax.ShapeDtypeStruct((tokens, (groups * heads + 2) * width), f32),
        in_specs=[whole()] * 6,
        out_specs=whole(),
        compiler_params=params,
        cost_estimate=pl.CostEstimate(
            flops=4 * tokens * tokens * groups * row_width,
            transcendentals=tokens * tokens * groups * heads,
            bytes_accessed=16 * tokens * groups * row_width,
        ),
        name="near",
    )(
        flat_queries,
        own_keys.reshape(tokens, groups * width),
        own_values.reshape(tokens, groups * width),
        turned,
        positions,
        positions.reshape(tokens, 1),
    )

    place = lax.axis_index("head").astype(jnp.int32).reshape(1)
    pieces = []
    for item, (first, count) in zip(back, PARTS):
        made = pl.pallas_call(
            lambda *refs: merge_kernel(first, groups, capacity, heads, width, *refs),
            out_shape=[jax.ShapeDtypeStruct((count, quarter, row_width), bf16)] * members,
            in_specs=[smem] + [whole()] * 2,
            out_specs=[whole()] * members,
            scratch_shapes=[pltpu.VMEM((tokens, row_width), f32)],
            compiler_params=small,
            name="merge",
        )(place, near, item)
        made = list(made)
        for step in ORDER:
            pairs = [(i, (i + step) % members) for i in range(members)]
            made[step] = lax.ppermute(made[step], "head", pairs)
        pieces += made
    joined = pl.pallas_call(
        lambda *refs: assemble_kernel(members, *refs),
        out_shape=jax.ShapeDtypeStruct((members, groups, quarter, row_width), bf16),
        in_specs=[smem] + [whole()] * len(pieces),
        out_specs=whole(),
        compiler_params=small,
        name="assemble",
    )(place, *pieces)
    joined = joined.reshape(members * groups, quarter, row_width)
    return jnp.transpose(joined, (1, 0, 2))


def solution(mesh):
    in_specs = (
        P("ctx", "head", None),
        P("ctx", "head", None),
        P("ctx", "head", None),
        P("ctx", "head", None),
        P("ctx", "head", None),
        P("head", "ctx", None),
        P("ctx", None),
    )
    out_specs = P(("ctx", "head"), None, None)
    return jax.shard_map(local, mesh=mesh, in_specs=in_specs, out_specs=out_specs, check_vma=False)
```

time: 175 us -> 167 us (0.954)
  waiting for transfers between devices: 85 us -> 71.9 us
  starting transfers between devices: 35.2 us -> 42 us
  local copies, waits for them, and re-layouts: 12.7 us -> 10.6 us
    all_to_all x1 -> x2, waiting for transfers between devices: 46.7 us -> 32.7 us  [local(): back = [lax.all_to_all(item, 'ctx', 0, 0, tiled=True) for item in parts]]
    ppermute x3 -> x6, starting transfers between devices: 5.05 us -> 10 us  [local(): made[step] = lax.ppermute(made[step], 'head', pairs)]
    all_to_all x2, waiting for transfers between devices: 33.3 us -> 36.6 us  [local(): received = [lax.all_to_all(item, 'ctx', 0, 0, tiled=True) for item in sent]]
    ppermute x3 -> x6, waiting for transfers between devices: 4.99 us -> 2.59 us  [local(): made[step] = lax.ppermute(made[step], 'head', pairs)]
    unnamed x23, local copies, waits for them, and re-layouts: 5.58 us -> 3.79 us
    all_to_all x1 -> x2, starting transfers between devices: 10.7 us -> 12.4 us  [local(): back = [lax.all_to_all(item, 'ctx', 0, 0, tiled=True) for item in parts]]
    pallas_call x4 -> x5, Pallas kernels: 30.7 us -> 31.3 us  [the longest x2 27 us: far(): pl.pallas_call(lambda *refs: far_kernel(scale, count, *refs), grid=(count...]
  transfers between devices with their start and end apart: 6 -> 10, of which waited for: 4 -> 6; matrix products, arithmetic and copies ran while one was open for 3% -> 3% of each run, Pallas kernels for 15% -> 24%
where the time goes in v3:
time: 167 us
  waiting for transfers between devices  71.9 us (43%)
  starting transfers between devices  42 us (25%)
  Pallas kernels  41.9 us (25%)
  local copies, waits for them, and re-layouts  10.6 us (6%)
    all_to_all x2, waiting for transfers between devices, local(): received = [lax.all_to_all(item, 'ctx', 0, 0, tiled=True) for item in sent]  36.6 us
    all_to_all x2, waiting for transfers between devices, local(): back = [lax.all_to_all(item, 'ctx', 0, 0, tiled=True) for item in parts]  32.7 us
    pallas_call x2, Pallas kernels, far(): pl.pallas_call(lambda *refs: far_kernel(scale, count, *refs), grid=(count...  27 us
    all_to_all x2, starting transfers between devices, local(): received = [lax.all_to_all(item, 'ctx', 0, 0, tiled=True) for item in sent]  19.6 us
    all_to_all x2, starting transfers between devices, local(): back = [lax.all_to_all(item, 'ctx', 0, 0, tiled=True) for item in parts]  12.4 us
    ppermute x6, starting transfers between devices, local(): made[step] = lax.ppermute(made[step], 'head', pairs)  10 us
    pallas_call x1, Pallas kernels, local(): pl.pallas_call(lambda *refs: near_kernel(sources, capacity, heads, width,...  5.7 us
    pallas_call x2, Pallas kernels, dispatch(): pl.pallas_call(lambda *refs: dispatch_kernel(first, sources, capacity, he...  4.93 us
  transfers between devices with their start and end apart: 10, of which 6 were waited for; matrix products, arithmetic and copies ran while one was open for 3% of the time, Pallas kernels for 24%

profile of v3, /device:TPU:1, one launch (start us, length us, event | category | flops | bytes accessed | tf_op | source)
XLA Modules:
  0.0 166.5 jit_solution(7491697521994999642)
XLA Ops:
  0.0 0.0 copy-start.6
  0.0 1.2 copy.10
  1.2 0.0 copy-start.2
  1.2 0.0 copy-start.5
  1.2 0.7 copy-done.5
  1.9 2.4 %dispatch.3 = bf16[64,2,32,128]{3,2,1,0:T(8,128)(2,1)} custom-call(bf16[128,2048]{1,0:T(8,128)(2,1)S(1)} %bitcast.21, s32[3,4,128]{2,1,0:T(4,128)S(1)} %bitcast.26), custom_call_target="tpu_custom_call" | custom-call | tf_op jit(solution)/shard_map/dispatch/pallas_call | solution.py:257
  4.3 13.2 %all-to-all-start.2 = ((bf16[64,2,32,128]{3,2,1,0:T(8,128)(2,1)}), bf16[64,2,32,128]{3,2,1,0:T(8,128)(2,1)}, u32[]{:S(2)}, u32[]{:S(2)}) async-start(bf16[64,2,32,128]{3,2,1,0:T(8,128)(2,1)} %dispatch.3), calls=%async_computation.2 | async-start | bytes 2097152 | tf_op jit(solution)/shard_map/all_to_all | solution.py:300
  17.5 0.0 copy-done.6
  17.5 0.0 copy-start.7
  17.5 2.5 %dispatch.2 = bf16[64,2,32,128]{3,2,1,0:T(8,128)(2,1)} custom-call(bf16[128,2048]{1,0:T(8,128)(2,1)S(1)} %bitcast.22, s32[3,4,128]{2,1,0:T(4,128)S(1)} %bitcast.27), custom_call_target="tpu_custom_call" | custom-call | tf_op jit(solution)/shard_map/dispatch/pallas_call | solution.py:257
  20.0 0.0 copy-done.2
  20.0 25.9 %all-to-all-done.2.refs_0_ = bf16[64,2,32,128]{3,2,1,0:T(8,128)(2,1)} async-done(((bf16[64,2,32,128]{3,2,1,0:T(8,128)(2,1)}), bf16[64,2,32,128]{3,2,1,0:T(8,128)(2,1)}, u32[]{:S(2)}, u32[]{:S(2)}) %all-to-all-start.2) | async-done | bytes 1048608 | tf_op jit(solution)/shard_map/all_to_all | solution.py:300
  46.0 6.4 %all-to-all-start = ((bf16[64,2,32,128]{3,2,1,0:T(8,128)(2,1)}), bf16[64,2,32,128]{3,2,1,0:T(8,128)(2,1)}, u32[]{:S(2)}, u32[]{:S(2)}) async-start(bf16[64,2,32,128]{3,2,1,0:T(8,128)(2,1)} %dispatch.2), calls=%async_computation | async-start | bytes 2097152 | tf_op jit(solution)/shard_map/all_to_all | solution.py:300
  52.4 0.0 copy-done.7
  52.4 4.2 %copy_bitcast_fusion = (bf16[2048,512]{1,0:T(8,128)(2,1)}, bf16[2048,512]{1,0:T(8,128)(2,1)}) fusion(bf16[256,8,4,128]{3,2,1,0:T(4,128)(2,1)S(1)} %bitcast.28, bf16[256,8,4,128]{3,2,1,0:T(4,128)(2,1)} %bitcast.29), kind=kLoop, calls=%fused_computation | loop fusion | bytes 8388608 | tf_op jit(solution)/shard_map/reshape | solution.py:269
  56.6 13.5 %far.3 = bf16[64,72,128]{2,1,0:T(8,128)(2,1)} custom-call(bf16[64,2,32,128]{3,2,1,0:T(8,128)(2,1)} %all-to-all-done.2.refs_0_, bf16[2048,512]{1,0:T(8,128)(2,1)} %get-tuple-element.30.refs_1_, bf16[2048,512]{1,0:T(8,128)(2,1)} %get-tuple-element.29.refs_2_), custom_call_target="tpu_custom_call" | custom-call | flops 6442450944 | bytes 2097152 | tf_op jit(solution)/shard_map/far/pallas_call | solution.py:277
  70.1 10.7 %all-to-all-done.refs_0_ = bf16[64,2,32,128]{3,2,1,0:T(8,128)(2,1)} async-done(((bf16[64,2,32,128]{3,2,1,0:T(8,128)(2,1)}), bf16[64,2,32,128]{3,2,1,0:T(8,128)(2,1)}, u32[]{:S(2)}, u32[]{:S(2)}) %all-to-all-start) | async-done | bytes 1048608 | tf_op jit(solution)/shard_map/all_to_all | solution.py:300
  80.8 6.2 %all-to-all-start.3 = ((bf16[64,72,128]{2,1,0:T(8,128)(2,1)}), bf16[64,72,128]{2,1,0:T(8,128)(2,1)S(1)}, u32[]{:S(2)}, u32[]{:S(2)}) async-start(bf16[64,72,128]{2,1,0:T(8,128)(2,1)} %far.3), calls=%async_computation.3 | async-start | bytes 2359296 | tf_op jit(solution)/shard_map/all_to_all | solution.py:302
  87.0 13.5 %far.2 = bf16[64,72,128]{2,1,0:T(8,128)(2,1)} custom-call(bf16[64,2,32,128]{3,2,1,0:T(8,128)(2,1)} %all-to-all-done.refs_0_, bf16[2048,512]{1,0:T(8,128)(2,1)} %get-tuple-element.30.refs_1_, bf16[2048,512]{1,0:T(8,128)(2,1)} %get-tuple-element.29.refs_2_), custom_call_target="tpu_custom_call" | custom-call | flops 6442450944 | bytes 2097152 | tf_op jit(solution)/shard_map/far/pallas_call | solution.py:277
  100.6 0.0 copy-start.10
  100.6 17.8 %all-to-all-done.3.refs_2_ = bf16[64,72,128]{2,1,0:T(8,128)(2,1)S(1)} async-done(((bf16[64,72,128]{2,1,0:T(8,128)(2,1)}), bf16[64,72,128]{2,1,0:T(8,128)(2,1)S(1)}, u32[]{:S(2)}, u32[]{:S(2)}) %all-to-all-start.3) | async-done | bytes 1179680 | tf_op jit(solution)/shard_map/all_to_all | solution.py:302
  118.4 6.2 %all-to-all-start.1 = ((bf16[64,72,128]{2,1,0:T(8,128)(2,1)}), bf16[64,72,128]{2,1,0:T(8,128)(2,1)S(1)}, u32[]{:S(2)}, u32[]{:S(2)}) async-start(bf16[64,72,128]{2,1,0:T(8,128)(2,1)} %far.2), calls=%async_computation.1 | async-start | bytes 2359296 | tf_op jit(solution)/shard_map/all_to_all | solution.py:302
  124.6 0.0 copy-done.10
  124.6 0.7 copy.8.refs_5_
  125.4 0.0 copy-done.8
  125.4 0.0 copy-done.9
  125.4 0.7 copy_bitcast_fusion.3
  126.1 5.7 %near.1.refs_1_ = f32[128,2304]{1,0:T(8,128)} custom-call(bf16[128,2048]{1,0:T(8,128)(2,1)} %bitcast.23, bf16[128,512]{1,0:T(8,128)(2,1)} %get-tuple-element.28.refs_1_, bf16[128,512]{1,0:T(8,128)(2,1)} %get-tuple-element.27.refs_2_, s32[3,4,128]{2,1,0:T(4,128)} %bitcast.25, s32[1,128]{1,0:T(1,128)} %refs_4_.1, s32[128,1]{1,0:T(8,128)} %copy.8.refs_5_), custom_call_target="tpu_custom_call" | custom-call | flops 134217728 | bytes 4194304 | tf_op jit(solution)/shard_map/near/pallas_call | solution.py:304
  131.8 1.3 copy-done
  133.1 2.4 %merge.3 = (bf16[2,32,512]{2,1,0:T(8,128)(2,1)S(1)}, bf16[2,32,512]{2,1,0:T(8,128)(2,1)}, bf16[2,32,512]{2,1,0:T(8,128)(2,1)}, bf16[2,32,512]{2,1,0:T(8,128)(2,1)}) custom-call(s32[1]{0:T(128)} %bitcast.refs_0_, f32[128,2304]{1,0:T(8,128)S(1)} %copy-done, bf16[64,72,128]{2,1,0:T(8,128)(2,1)S(1)} %all-to-all-done.3.refs_2_), custom_call_target="tpu_custom_call" | custom-call | tf_op jit(solution)/shard_map/merge/pallas_call | solution.py:328
  135.5 0.6 copy-done.3
  136.1 1.3 collective-permute-start.3
  137.4 2.6 %collective-permute-start.4 = (bf16[2,32,512]{2,1,0:T(8,128)(2,1)}, bf16[2,32,512]{2,1,0:T(8,128)(2,1)S(1)}, u32[]{:S(2)}, u32[]{:S(2)}) collective-permute-start(bf16[2,32,512]{2,1,0:T(8,128)(2,1)} %get-tuple-element.25), channel_id=1, source_target_pairs={{0,2},{1,3},{2,0},{3,1},{4,6},{5,7},{6,4},{7,5},{8,10},{9,11},{10,... | collective-permute-start | bytes 196616 | tf_op jit(solution)/shard_map/ppermute | solution.py:340
  140.1 1.1 collective-permute-start.5
  141.1 14.8 %all-to-all-done.1.refs_2_ = bf16[64,72,128]{2,1,0:T(8,128)(2,1)S(1)} async-done(((bf16[64,72,128]{2,1,0:T(8,128)(2,1)}), bf16[64,72,128]{2,1,0:T(8,128)(2,1)S(1)}, u32[]{:S(2)}, u32[]{:S(2)}) %all-to-all-start.1) | async-done | bytes 1179680 | tf_op jit(solution)/shard_map/all_to_all | solution.py:302
  156.0 0.0 copy-done.1
  156.0 1.8 %merge.2 = (bf16[2,32,512]{2,1,0:T(8,128)(2,1)S(1)}, bf16[2,32,512]{2,1,0:T(8,128)(2,1)S(1)}, bf16[2,32,512]{2,1,0:T(8,128)(2,1)S(1)}, bf16[2,32,512]{2,1,0:T(8,128)(2,1)S(1)}) custom-call(s32[1]{0:T(128)} %bitcast.refs_0_, f32[128,2304]{1,0:T(8,128)S(1)} %copy-done.1, bf16[64,72,128]{2,1,0:T(8,128)(2,1)S(1)} %all-to-all-done.1.refs_2_), custom_call_target="tpu_custom_call" | custom-call | tf_op jit(solution)/shard_map/merge/pallas_call | solution.py:328
  157.8 1.4 collective-permute-start
  159.1 2.6 %collective-permute-start.1 = (bf16[2,32,512]{2,1,0:T(8,128)(2,1)S(1)}, bf16[2,32,512]{2,1,0:T(8,128)(2,1)S(1)}, u32[]{:S(2)}, u32[]{:S(2)}) collective-permute-start(bf16[2,32,512]{2,1,0:T(8,128)(2,1)S(1)} %get-tuple-element.20), channel_id=1, source_target_pairs={{0,2},{1,3},{2,0},{3,1},{4,6},{5,7},{6,4},{7,5},{8,10},{9,11},{10,... | collective-permute-start | bytes 196616 | tf_op jit(solution)/shard_map/ppermute | solution.py:340
  161.7 0.0 collective-permute-done.3.refs_6_
  161.8 1.1 collective-permute-start.2
  162.8 0.0 collective-permute-done.4.refs_7_
  162.8 0.0 collective-permute-done.5.refs_8_
  162.8 0.1 collective-permute-done.refs_2_
  162.9 2.5 %collective-permute-done.1.refs_3_ = bf16[2,32,512]{2,1,0:T(8,128)(2,1)S(1)} collective-permute-done((bf16[2,32,512]{2,1,0:T(8,128)(2,1)S(1)}, bf16[2,32,512]{2,1,0:T(8,128)(2,1)S(1)}, u32[]{:S(2)}, u32[]{:S(2)}) %collective-permute-start.1) | collective-permute-done | bytes 65568 | tf_op jit(solution)/shard_map/ppermute | solution.py:340
  165.4 0.0 collective-permute-done.2.refs_4_
  165.4 0.0 copy-done.4
  165.5 1.1 copy.20
  (7 shorter events, 0.0 us)
Async XLA Ops:
  0.0 17.5 %copy-start.6 = (s32[4,128,3]{1,0,2:T(4,128)S(1)}, s32[4,128,3]{1,0,2:T(4,128)}, u32[]{:S(2)}) copy-start(s32[4,128,3]{1,0,2:T(4,128)} %param.12) | copy-start | bytes 18436
  1.2 18.9 %copy-start.2 = (bf16[16,8,4,512]{3,1,2,0:T(8,128)(2,1)}, bf16[16,8,4,512]{3,1,2,0:T(8,128)(2,1)S(1)}, u32[]{:S(2)}) copy-start(bf16[16,8,4,512]{3,1,2,0:T(8,128)(2,1)S(1)} %copy.10) | copy-start | bytes 1572868
  1.2 0.7 copy-start.5
  4.3 41.7 %all-to-all-start.2 = ((bf16[64,2,32,128]{3,2,1,0:T(8,128)(2,1)}), bf16[64,2,32,128]{3,2,1,0:T(8,128)(2,1)}, u32[]{:S(2)}, u32[]{:S(2)}) async-start(bf16[64,2,32,128]{3,2,1,0:T(8,128)(2,1)} %dispatch.3), calls=%async_computation.2 | async-start | bytes 2097152 | tf_op jit(solution)/shard_map/all_to_all | solution.py:300
  17.5 34.9 %copy-start.7 = (bf16[2048,4,128]{2,1,0:T(4,128)(2,1)S(1)}, bf16[2048,4,128]{2,1,0:T(4,128)(2,1)}, u32[]{:S(2)}) copy-start(bf16[2048,4,128]{2,1,0:T(4,128)(2,1)} %param.9) | copy-start | bytes 6291460
  46.0 34.9 %all-to-all-start = ((bf16[64,2,32,128]{3,2,1,0:T(8,128)(2,1)}), bf16[64,2,32,128]{3,2,1,0:T(8,128)(2,1)}, u32[]{:S(2)}, u32[]{:S(2)}) async-start(bf16[64,2,32,128]{3,2,1,0:T(8,128)(2,1)} %dispatch.2), calls=%async_computation | async-start | bytes 2097152 | tf_op jit(solution)/shard_map/all_to_all | solution.py:300
  80.8 37.6 %all-to-all-start.3 = ((bf16[64,72,128]{2,1,0:T(8,128)(2,1)}), bf16[64,72,128]{2,1,0:T(8,128)(2,1)S(1)}, u32[]{:S(2)}, u32[]{:S(2)}) async-start(bf16[64,72,128]{2,1,0:T(8,128)(2,1)} %far.3), calls=%async_computation.3 | async-start | bytes 2359296 | tf_op jit(solution)/shard_map/all_to_all | solution.py:302
  100.6 24.0 %copy-start.10 = (s32[1,128]{1,0:T(1,128)S(1)}, s32[1,128]{1,0:T(1,128)}, u32[]{:S(2)}) copy-start(s32[1,128]{1,0:T(1,128)} %refs_4_.1) | copy-start | bytes 1540
  100.6 24.8 %copy-start.8 = (bf16[128,4,128]{2,1,0:T(4,128)(2,1)S(1)}, bf16[128,4,128]{2,1,0:T(4,128)(2,1)}, u32[]{:S(2)}) copy-start(bf16[128,4,128]{2,1,0:T(4,128)(2,1)} %param.11) | copy-start | bytes 393220
  100.6 24.8 %copy-start.9 = (bf16[128,4,128]{2,1,0:T(4,128)(2,1)S(1)}, bf16[128,4,128]{2,1,0:T(4,128)(2,1)}, u32[]{:S(2)}) copy-start(bf16[128,4,128]{2,1,0:T(4,128)(2,1)} %param.10) | copy-start | bytes 393220
  118.4 37.6 %all-to-all-start.1 = ((bf16[64,72,128]{2,1,0:T(8,128)(2,1)}), bf16[64,72,128]{2,1,0:T(8,128)(2,1)S(1)}, u32[]{:S(2)}, u32[]{:S(2)}) async-start(bf16[64,72,128]{2,1,0:T(8,128)(2,1)} %far.2), calls=%async_computation.1 | async-start | bytes 2359296 | tf_op jit(solution)/shard_map/all_to_all | solution.py:302
  131.8 1.3 copy-start
  133.1 22.9 %copy-start.1 = (f32[128,2304]{1,0:T(8,128)S(1)}, f32[128,2304]{1,0:T(8,128)}, u32[]{:S(2)}) copy-start(f32[128,2304]{1,0:T(8,128)} %near.1.refs_1_) | copy-start | bytes 3538948
  135.5 0.6 copy-start.3
  136.1 29.3 %copy-start.4 = (bf16[2,32,512]{2,1,0:T(8,128)(2,1)S(1)}, bf16[2,32,512]{2,1,0:T(8,128)(2,1)}, u32[]{:S(2)}) copy-start(bf16[2,32,512]{2,1,0:T(8,128)(2,1)} %copy-done.3) | copy-start | bytes 196612
  136.1 25.6 %collective-permute-start.3 = (bf16[2,32,512]{2,1,0:T(8,128)(2,1)}, bf16[2,32,512]{2,1,0:T(8,128)(2,1)S(1)}, u32[]{:S(2)}, u32[]{:S(2)}) collective-permute-start(bf16[2,32,512]{2,1,0:T(8,128)(2,1)} %get-tuple-element.24), channel_id=1, source_target_pairs={{0,1},{1,2},{2,3},{3,0},{4,5},{5,6},{6,7},{7,4},{8,9},{9,10},{10,1... | collective-permute-start | bytes 196616 | tf_op jit(solution)/shard_map/ppermute | solution.py:340
  137.4 25.4 %collective-permute-start.4 = (bf16[2,32,512]{2,1,0:T(8,128)(2,1)}, bf16[2,32,512]{2,1,0:T(8,128)(2,1)S(1)}, u32[]{:S(2)}, u32[]{:S(2)}) collective-permute-start(bf16[2,32,512]{2,1,0:T(8,128)(2,1)} %get-tuple-element.25), channel_id=1, source_target_pairs={{0,2},{1,3},{2,0},{3,1},{4,6},{5,7},{6,4},{7,5},{8,10},{9,11},{10,... | collective-permute-start | bytes 196616 | tf_op jit(solution)/shard_map/ppermute | solution.py:340
  140.1 22.8 %collective-permute-start.5 = (bf16[2,32,512]{2,1,0:T(8,128)(2,1)}, bf16[2,32,512]{2,1,0:T(8,128)(2,1)S(1)}, u32[]{:S(2)}, u32[]{:S(2)}) collective-permute-start(bf16[2,32,512]{2,1,0:T(8,128)(2,1)} %get-tuple-element.26), channel_id=1, source_target_pairs={{0,3},{1,0},{2,1},{3,2},{4,7},{5,4},{6,5},{7,6},{8,11},{9,8},{10,9... | collective-permute-start | bytes 196616 | tf_op jit(solution)/shard_map/ppermute | solution.py:340
  157.8 5.1 %collective-permute-start = (bf16[2,32,512]{2,1,0:T(8,128)(2,1)S(1)}, bf16[2,32,512]{2,1,0:T(8,128)(2,1)S(1)}, u32[]{:S(2)}, u32[]{:S(2)}) collective-permute-start(bf16[2,32,512]{2,1,0:T(8,128)(2,1)S(1)} %get-tuple-element.19), channel_id=1, source_target_pairs={{0,1},{1,2},{2,3},{3,0},{4,5},{5,6},{6,7},{7,4},{8,9},{9,10},{10,1... | collective-permute-start | bytes 196616 | tf_op jit(solution)/shard_map/ppermute | solution.py:340
  159.1 6.3 %collective-permute-start.1 = (bf16[2,32,512]{2,1,0:T(8,128)(2,1)S(1)}, bf16[2,32,512]{2,1,0:T(8,128)(2,1)S(1)}, u32[]{:S(2)}, u32[]{:S(2)}) collective-permute-start(bf16[2,32,512]{2,1,0:T(8,128)(2,1)S(1)} %get-tuple-element.20), channel_id=1, source_target_pairs={{0,2},{1,3},{2,0},{3,1},{4,6},{5,7},{6,4},{7,5},{8,10},{9,11},{10,... | collective-permute-start | bytes 196616 | tf_op jit(solution)/shard_map/ppermute | solution.py:340
  161.8 3.7 %collective-permute-start.2 = (bf16[2,32,512]{2,1,0:T(8,128)(2,1)S(1)}, bf16[2,32,512]{2,1,0:T(8,128)(2,1)S(1)}, u32[]{:S(2)}, u32[]{:S(2)}) collective-permute-start(bf16[2,32,512]{2,1,0:T(8,128)(2,1)S(1)} %get-tuple-element.21), channel_id=1, source_target_pairs={{0,3},{1,0},{2,1},{3,2},{4,7},{5,4},{6,5},{7,6},{8,11},{9,8},{10,9... | collective-permute-start | bytes 196616 | tf_op jit(solution)/shard_map/ppermute | solution.py:340

commit v4 on v3

--- a/solution.py
+++ b/solution.py
@@ -224,11 +224,13 @@
 
 
 def assemble_kernel(count, place_ref, *refs):
-    piece_refs, out_ref = refs[:-1], refs[-1]
+    piece_refs, out_ref, row_ref = refs[:-2], refs[-2], refs[-1]
+    groups = row_ref.shape[0] // count
     for i, piece_ref in enumerate(piece_refs):
         origin = lax.rem(place_ref[0] + count - i % count, count)
-        first = PARTS[i // count][0]
-        out_ref[origin, first : first + piece_ref.shape[0]] = piece_ref[...]
+        first = origin * groups + PARTS[i // count][0]
+        row_ref[pl.ds(first, piece_ref.shape[0])] = piece_ref[...].astype(jnp.float32)
+    out_ref[...] = jnp.swapaxes(row_ref[...], 0, 1).astype(out_ref.dtype)
 
 
 def local(queries, hist_keys, hist_values, own_keys, own_values, choices, positions):
@@ -299,7 +301,10 @@
 
     received = [lax.all_to_all(item, "ctx", 0, 0, tiled=True) for item in sent]
     parts = [far(item, *part) for item, part in zip(received, PARTS)]
+    rows = PARTS[0][1] * per_source + LSE_ROWS // 2
+    parts[0] = parts[0][:, :rows].reshape(sources, rows // 4, 4, width)
     back = [lax.all_to_all(item, "ctx", 0, 0, tiled=True) for item in parts]
+    back[0] = back[0].reshape(sources, rows, width)
 
     near = pl.pallas_call(
         lambda *refs: near_kernel(sources, capacity, heads, width, scale, *refs),
@@ -339,16 +344,15 @@
             pairs = [(i, (i + step) % members) for i in range(members)]
             made[step] = lax.ppermute(made[step], "head", pairs)
         pieces += made
-    joined = pl.pallas_call(
+    return pl.pallas_call(
         lambda *refs: assemble_kernel(members, *refs),
-        out_shape=jax.ShapeDtypeStruct((members, groups, quarter, row_width), bf16),
+        out_shape=jax.ShapeDtypeStruct((quarter, members * groups, row_width), bf16),
         in_specs=[smem] + [whole()] * len(pieces),
         out_specs=whole(),
+        scratch_shapes=[pltpu.VMEM((members * groups, quarter, row_width), f32)],
         compiler_params=small,
         name="assemble",
     )(place, *pieces)
-    joined = joined.reshape(members * groups, quarter, row_width)
-    return jnp.transpose(joined, (1, 0, 2))
 
 
 def solution(mesh):

time: 167 us -> 167 us (level)
  waiting for transfers between devices: 71.9 us -> 68.2 us
  local copies, waits for them, and re-layouts: 10.6 us -> 13.5 us
    all_to_all x2, waiting for transfers between devices: 36.6 us -> 33.5 us  [local(): received = [lax.all_to_all(item, 'ctx', 0, 0, tiled=True) for item in sent]]
    unnamed x23 -> x21, local copies, waits for them, and re-layouts: 3.79 us -> 3.4 us
  transfers between devices with their start and end apart: 10 -> 10, of which waited for: 6 -> 6; matrix products, arithmetic and copies ran while one was open for 3% -> 6% of each run, Pallas kernels for 24% -> 23%
where the time goes in v4:
time: 167 us; the launch traced here: 166 us
  waiting for transfers between devices  68.2 us (41%)
  Pallas kernels  42.2 us (25%)
  starting transfers between devices  42 us (25%)
  local copies, waits for them, and re-layouts  13.5 us (8%)
    all_to_all x2, waiting for transfers between devices, local(): received = [lax.all_to_all(item, 'ctx', 0, 0, tiled=True) for item in sent]  33.5 us
    all_to_all x2, waiting for transfers between devices, local(): back = [lax.all_to_all(item, 'ctx', 0, 0, tiled=True) for item in parts]  32.2 us
    pallas_call x2, Pallas kernels, far(): pl.pallas_call(lambda *refs: far_kernel(scale, count, *refs), grid=(count...  27.1 us
    all_to_all x2, starting transfers between devices, local(): received = [lax.all_to_all(item, 'ctx', 0, 0, tiled=True) for item in sent]  19.3 us
    all_to_all x2, starting transfers between devices, local(): back = [lax.all_to_all(item, 'ctx', 0, 0, tiled=True) for item in parts]  12.6 us
    ppermute x6, starting transfers between devices, local(): made[step] = lax.ppermute(made[step], 'head', pairs)  10.1 us
    pallas_call x1, Pallas kernels, local(): pl.pallas_call(lambda *refs: near_kernel(sources, capacity, heads, width,...  5.69 us
    pallas_call x2, Pallas kernels, dispatch(): pl.pallas_call(lambda *refs: dispatch_kernel(first, sources, capacity, he...  4.87 us
  transfers between devices with their start and end apart: 10, of which 6 were waited for; matrix products, arithmetic and copies ran while one was open for 6% of the time, Pallas kernels for 23%

profile of v4, /device:TPU:1, one launch (start us, length us, event | category | flops | bytes accessed | tf_op | source)
XLA Modules:
  0.0 166.2 jit_solution(17614543820251054019)
XLA Ops:
  0.0 1.1 copy.17
  1.1 0.0 copy-start.1
  1.2 0.0 copy-start.2
  1.2 0.7 copy-done.2
  1.9 2.5 %dispatch.2 = bf16[64,2,32,128]{3,2,1,0:T(8,128)(2,1)} custom-call(bf16[128,2048]{1,0:T(8,128)(2,1)S(1)} %bitcast.20, s32[3,4,128]{2,1,0:T(4,128)S(1)} %bitcast.24), custom_call_target="tpu_custom_call" | custom-call | tf_op jit(solution)/shard_map/dispatch/pallas_call | solution.py:259
  4.3 13.1 %all-to-all-start = ((bf16[64,2,32,128]{3,2,1,0:T(8,128)(2,1)}), bf16[64,2,32,128]{3,2,1,0:T(8,128)(2,1)S(1)}, u32[]{:S(2)}, u32[]{:S(2)}) async-start(bf16[64,2,32,128]{3,2,1,0:T(8,128)(2,1)} %dispatch.2), calls=%async_computation | async-start | bytes 2097152 | tf_op jit(solution)/shard_map/all_to_all | solution.py:302
  17.5 0.0 copy-done.1
  17.5 0.0 copy-done.3
  17.5 2.4 %dispatch.3 = bf16[64,2,32,128]{3,2,1,0:T(8,128)(2,1)} custom-call(bf16[128,2048]{1,0:T(8,128)(2,1)S(1)} %bitcast.21, s32[3,4,128]{2,1,0:T(4,128)S(1)} %bitcast.25), custom_call_target="tpu_custom_call" | custom-call | tf_op jit(solution)/shard_map/dispatch/pallas_call | solution.py:259
  19.9 26.1 %all-to-all-done.refs_0_ = bf16[64,2,32,128]{3,2,1,0:T(8,128)(2,1)S(1)} async-done(((bf16[64,2,32,128]{3,2,1,0:T(8,128)(2,1)}), bf16[64,2,32,128]{3,2,1,0:T(8,128)(2,1)S(1)}, u32[]{:S(2)}, u32[]{:S(2)}) %all-to-all-start) | async-done | bytes 1048608 | tf_op jit(solution)/shard_map/all_to_all | solution.py:302
  46.0 1.0 copy-done.6
  47.0 6.2 %all-to-all-start.2 = ((bf16[64,2,32,128]{3,2,1,0:T(8,128)(2,1)}), bf16[64,2,32,128]{3,2,1,0:T(8,128)(2,1)S(1)}, u32[]{:S(2)}, u32[]{:S(2)}) async-start(bf16[64,2,32,128]{3,2,1,0:T(8,128)(2,1)} %dispatch.3), calls=%async_computation.2 | async-start | bytes 2097152 | tf_op jit(solution)/shard_map/all_to_all | solution.py:302
  53.2 0.0 copy-done.4
  53.2 4.2 %copy_bitcast_fusion = (bf16[2048,512]{1,0:T(8,128)(2,1)}, bf16[2048,512]{1,0:T(8,128)(2,1)}) fusion(bf16[256,8,4,128]{3,2,1,0:T(4,128)(2,1)S(1)} %bitcast.28, bf16[256,8,4,128]{3,2,1,0:T(4,128)(2,1)} %bitcast.29), kind=kLoop, calls=%fused_computation | loop fusion | bytes 8388608 | tf_op jit(solution)/shard_map/reshape | solution.py:271
  57.5 13.5 %far.2 = bf16[64,72,128]{2,1,0:T(8,128)(2,1)} custom-call(bf16[64,2,32,128]{3,2,1,0:T(8,128)(2,1)} %copy-done.6, bf16[2048,512]{1,0:T(8,128)(2,1)} %get-tuple-element.30.refs_1_, bf16[2048,512]{1,0:T(8,128)(2,1)} %get-tuple-element.29.refs_2_), custom_call_target="tpu_custom_call" | custom-call | flops 6442450944 | bytes 2097152 | tf_op jit(solution)/shard_map/far/pallas_call | solution.py:279
  71.0 1.5 copy.13
  72.5 1.9 %copy.14 = bf16[64,17,4,128]{3,2,1,0:T(4,128)(2,1)} copy(bf16[64,17,4,128]{3,0,2,1:T(8,128)(2,1)S(1)} %bitcast.26) | data formatting | bytes 2228224 | tf_op jit(solution)/shard_map/reshape | solution.py:305
  74.4 7.3 %all-to-all-done.2.refs_0_ = bf16[64,2,32,128]{3,2,1,0:T(8,128)(2,1)S(1)} async-done(((bf16[64,2,32,128]{3,2,1,0:T(8,128)(2,1)}), bf16[64,2,32,128]{3,2,1,0:T(8,128)(2,1)S(1)}, u32[]{:S(2)}, u32[]{:S(2)}) %all-to-all-start.2) | async-done | bytes 1048608 | tf_op jit(solution)/shard_map/all_to_all | solution.py:302
  81.8 6.4 %all-to-all-start.1 = ((bf16[64,17,4,128]{3,2,1,0:T(4,128)(2,1)}), bf16[64,17,4,128]{3,2,1,0:T(4,128)(2,1)S(1)}, u32[]{:S(2)}, u32[]{:S(2)}) async-start(bf16[64,17,4,128]{3,2,1,0:T(4,128)(2,1)} %copy.14), calls=%async_computation.1 | async-start | bytes 2228224 | tf_op jit(solution)/shard_map/all_to_all | solution.py:306
  88.2 0.0 copy-done.5
  88.2 13.6 %far.3 = bf16[64,72,128]{2,1,0:T(8,128)(2,1)} custom-call(bf16[64,2,32,128]{3,2,1,0:T(8,128)(2,1)} %copy-done.5, bf16[2048,512]{1,0:T(8,128)(2,1)} %get-tuple-element.30.refs_1_, bf16[2048,512]{1,0:T(8,128)(2,1)} %get-tuple-element.29.refs_2_), custom_call_target="tpu_custom_call" | custom-call | flops 6442450944 | bytes 2097152 | tf_op jit(solution)/shard_map/far/pallas_call | solution.py:279
  101.7 16.4 %all-to-all-done.1 = bf16[64,17,4,128]{3,2,1,0:T(4,128)(2,1)S(1)} async-done(((bf16[64,17,4,128]{3,2,1,0:T(4,128)(2,1)}), bf16[64,17,4,128]{3,2,1,0:T(4,128)(2,1)S(1)}, u32[]{:S(2)}, u32[]{:S(2)}) %all-to-all-start.1) | async-done | bytes 1114144 | tf_op jit(solution)/shard_map/all_to_all | solution.py:306
  118.1 6.2 %all-to-all-start.3 = ((bf16[64,72,128]{2,1,0:T(8,128)(2,1)}), bf16[64,72,128]{2,1,0:T(8,128)(2,1)S(1)}, u32[]{:S(2)}, u32[]{:S(2)}) async-start(bf16[64,72,128]{2,1,0:T(8,128)(2,1)} %far.3), calls=%async_computation.3 | async-start | bytes 2359296 | tf_op jit(solution)/shard_map/all_to_all | solution.py:306
  124.3 0.0 copy-done.9
  124.3 0.7 copy.12.refs_5_
  125.1 0.0 copy-done.7
  125.1 0.0 copy-done.8
  125.1 0.7 copy_bitcast_fusion.2
  125.8 5.7 %near.1.refs_1_ = f32[128,2304]{1,0:T(8,128)} custom-call(bf16[128,2048]{1,0:T(8,128)(2,1)} %bitcast.22, bf16[128,512]{1,0:T(8,128)(2,1)} %get-tuple-element.28.refs_1_, bf16[128,512]{1,0:T(8,128)(2,1)} %get-tuple-element.27.refs_2_, s32[3,4,128]{2,1,0:T(4,128)} %bitcast.23, s32[1,128]{1,0:T(1,128)} %refs_4_.1, s32[128,1]{1,0:T(8,128)} %copy.12.refs_5_), custom_call_target="tpu_custom_call" | custom-call | flops 134217728 | bytes 4194304 | tf_op jit(solution)/shard_map/near/pallas_call | solution.py:309
  131.5 0.3 copy.15
  131.8 0.7 copy.16.refs_2_
  132.5 0.5 copy-done
  133.1 1.8 %merge.2 = (bf16[2,32,512]{2,1,0:T(8,128)(2,1)S(1)}, bf16[2,32,512]{2,1,0:T(8,128)(2,1)S(1)}, bf16[2,32,512]{2,1,0:T(8,128)(2,1)S(1)}, bf16[2,32,512]{2,1,0:T(8,128)(2,1)S(1)}) custom-call(s32[1]{0:T(128)} %bitcast.refs_0_, f32[128,2304]{1,0:T(8,128)S(1)} %copy-done, bf16[64,68,128]{2,1,0:T(8,128)(2,1)S(1)} %copy.16.refs_2_), custom_call_target="tpu_custom_call" | custom-call | tf_op jit(solution)/shard_map/merge/pallas_call | solution.py:333
  134.8 1.4 collective-permute-start
  136.2 2.6 %collective-permute-start.1 = (bf16[2,32,512]{2,1,0:T(8,128)(2,1)S(1)}, bf16[2,32,512]{2,1,0:T(8,128)(2,1)S(1)}, u32[]{:S(2)}, u32[]{:S(2)}) collective-permute-start(bf16[2,32,512]{2,1,0:T(8,128)(2,1)S(1)} %get-tuple-element.20), channel_id=1, source_target_pairs={{0,2},{1,3},{2,0},{3,1},{4,6},{5,7},{6,4},{7,5},{8,10},{9,11},{10,... | collective-permute-start | bytes 196616 | tf_op jit(solution)/shard_map/ppermute | solution.py:345
  138.8 1.1 collective-permute-start.2
  139.9 15.8 %all-to-all-done.3.refs_2_ = bf16[64,72,128]{2,1,0:T(8,128)(2,1)S(1)} async-done(((bf16[64,72,128]{2,1,0:T(8,128)(2,1)}), bf16[64,72,128]{2,1,0:T(8,128)(2,1)S(1)}, u32[]{:S(2)}, u32[]{:S(2)}) %all-to-all-start.3) | async-done | bytes 1179680 | tf_op jit(solution)/shard_map/all_to_all | solution.py:306
  155.7 1.8 %merge.3 = (bf16[2,32,512]{2,1,0:T(8,128)(2,1)S(1)}, bf16[2,32,512]{2,1,0:T(8,128)(2,1)S(1)}, bf16[2,32,512]{2,1,0:T(8,128)(2,1)S(1)}, bf16[2,32,512]{2,1,0:T(8,128)(2,1)S(1)}) custom-call(s32[1]{0:T(128)} %bitcast.refs_0_, f32[128,2304]{1,0:T(8,128)S(1)} %copy-done, bf16[64,72,128]{2,1,0:T(8,128)(2,1)S(1)} %all-to-all-done.3.refs_2_), custom_call_target="tpu_custom_call" | custom-call | tf_op jit(solution)/shard_map/merge/pallas_call | solution.py:333
  157.5 1.4 collective-permute-start.3
  158.8 2.6 %collective-permute-start.4 = (bf16[2,32,512]{2,1,0:T(8,128)(2,1)S(1)}, bf16[2,32,512]{2,1,0:T(8,128)(2,1)S(1)}, u32[]{:S(2)}, u32[]{:S(2)}) collective-permute-start(bf16[2,32,512]{2,1,0:T(8,128)(2,1)S(1)} %get-tuple-element.25), channel_id=1, source_target_pairs={{0,2},{1,3},{2,0},{3,1},{4,6},{5,7},{6,4},{7,5},{8,10},{9,11},{10,... | collective-permute-start | bytes 196616 | tf_op jit(solution)/shard_map/ppermute | solution.py:345
  161.5 0.0 collective-permute-done.refs_2_
  161.5 1.1 collective-permute-start.5
  162.5 0.0 collective-permute-done.1.refs_3_
  162.5 0.0 collective-permute-done.2.refs_4_
  162.5 0.1 collective-permute-done.3.refs_6_
  162.6 2.5 %collective-permute-done.4.refs_7_ = bf16[2,32,512]{2,1,0:T(8,128)(2,1)S(1)} collective-permute-done((bf16[2,32,512]{2,1,0:T(8,128)(2,1)S(1)}, bf16[2,32,512]{2,1,0:T(8,128)(2,1)S(1)}, u32[]{:S(2)}, u32[]{:S(2)}) %collective-permute-start.4) | collective-permute-done | bytes 65568 | tf_op jit(solution)/shard_map/ppermute | solution.py:345
  165.1 0.0 collective-permute-done.5.refs_8_
  165.1 1.1 assemble.1
  (8 shorter events, 0.0 us)
Async XLA Ops:
  1.1 16.3 %copy-start.1 = (bf16[16,8,4,512]{3,1,2,0:T(8,128)(2,1)}, bf16[16,8,4,512]{3,1,2,0:T(8,128)(2,1)S(1)}, u32[]{:S(2)}) copy-start(bf16[16,8,4,512]{3,1,2,0:T(8,128)(2,1)S(1)} %copy.17) | copy-start | bytes 1572868
  1.2 0.7 copy-start.2
  4.3 13.1 %copy-start.3 = (s32[4,128,3]{1,0,2:T(4,128)S(1)}, s32[4,128,3]{1,0,2:T(4,128)}, u32[]{:S(2)}) copy-start(s32[4,128,3]{1,0,2:T(4,128)} %param.12) | copy-start | bytes 18436
  4.3 41.7 %all-to-all-start = ((bf16[64,2,32,128]{3,2,1,0:T(8,128)(2,1)}), bf16[64,2,32,128]{3,2,1,0:T(8,128)(2,1)S(1)}, u32[]{:S(2)}, u32[]{:S(2)}) async-start(bf16[64,2,32,128]{3,2,1,0:T(8,128)(2,1)} %dispatch.2), calls=%async_computation | async-start | bytes 2097152 | tf_op jit(solution)/shard_map/all_to_all | solution.py:302
  19.9 33.3 %copy-start.4 = (bf16[2048,4,128]{2,1,0:T(4,128)(2,1)S(1)}, bf16[2048,4,128]{2,1,0:T(4,128)(2,1)}, u32[]{:S(2)}) copy-start(bf16[2048,4,128]{2,1,0:T(4,128)(2,1)} %param.9) | copy-start | bytes 6291460
  46.0 1.0 copy-start.6
  47.0 34.8 %all-to-all-start.2 = ((bf16[64,2,32,128]{3,2,1,0:T(8,128)(2,1)}), bf16[64,2,32,128]{3,2,1,0:T(8,128)(2,1)S(1)}, u32[]{:S(2)}, u32[]{:S(2)}) async-start(bf16[64,2,32,128]{3,2,1,0:T(8,128)(2,1)} %dispatch.3), calls=%async_computation.2 | async-start | bytes 2097152 | tf_op jit(solution)/shard_map/all_to_all | solution.py:302
  81.8 6.4 %copy-start.5 = (bf16[64,2,32,128]{3,2,1,0:T(8,128)(2,1)}, bf16[64,2,32,128]{3,2,1,0:T(8,128)(2,1)S(1)}, u32[]{:S(2)}) copy-start(bf16[64,2,32,128]{3,2,1,0:T(8,128)(2,1)S(1)} %all-to-all-done.2.refs_0_) | copy-start | bytes 3145732
  81.8 36.3 %all-to-all-start.1 = ((bf16[64,17,4,128]{3,2,1,0:T(4,128)(2,1)}), bf16[64,17,4,128]{3,2,1,0:T(4,128)(2,1)S(1)}, u32[]{:S(2)}, u32[]{:S(2)}) async-start(bf16[64,17,4,128]{3,2,1,0:T(4,128)(2,1)} %copy.14), calls=%async_computation.1 | async-start | bytes 2228224 | tf_op jit(solution)/shard_map/all_to_all | solution.py:306
  101.7 22.6 %copy-start.9 = (s32[1,128]{1,0:T(1,128)S(1)}, s32[1,128]{1,0:T(1,128)}, u32[]{:S(2)}) copy-start(s32[1,128]{1,0:T(1,128)} %refs_4_.1) | copy-start | bytes 1540
  101.7 23.4 %copy-start.7 = (bf16[128,4,128]{2,1,0:T(4,128)(2,1)S(1)}, bf16[128,4,128]{2,1,0:T(4,128)(2,1)}, u32[]{:S(2)}) copy-start(bf16[128,4,128]{2,1,0:T(4,128)(2,1)} %param.11) | copy-start | bytes 393220
  101.7 23.4 %copy-start.8 = (bf16[128,4,128]{2,1,0:T(4,128)(2,1)S(1)}, bf16[128,4,128]{2,1,0:T(4,128)(2,1)}, u32[]{:S(2)}) copy-start(bf16[128,4,128]{2,1,0:T(4,128)(2,1)} %param.10) | copy-start | bytes 393220
  118.1 37.6 %all-to-all-start.3 = ((bf16[64,72,128]{2,1,0:T(8,128)(2,1)}), bf16[64,72,128]{2,1,0:T(8,128)(2,1)S(1)}, u32[]{:S(2)}, u32[]{:S(2)}) async-start(bf16[64,72,128]{2,1,0:T(8,128)(2,1)} %far.3), calls=%async_computation.3 | async-start | bytes 2359296 | tf_op jit(solution)/shard_map/all_to_all | solution.py:306
  131.8 1.3 copy-start
  134.8 26.6 %collective-permute-start = (bf16[2,32,512]{2,1,0:T(8,128)(2,1)S(1)}, bf16[2,32,512]{2,1,0:T(8,128)(2,1)S(1)}, u32[]{:S(2)}, u32[]{:S(2)}) collective-permute-start(bf16[2,32,512]{2,1,0:T(8,128)(2,1)S(1)} %get-tuple-element.19), channel_id=1, source_target_pairs={{0,1},{1,2},{2,3},{3,0},{4,5},{5,6},{6,7},{7,4},{8,9},{9,10},{10,1... | collective-permute-start | bytes 196616 | tf_op jit(solution)/shard_map/ppermute | solution.py:345
  136.2 26.3 %collective-permute-start.1 = (bf16[2,32,512]{2,1,0:T(8,128)(2,1)S(1)}, bf16[2,32,512]{2,1,0:T(8,128)(2,1)S(1)}, u32[]{:S(2)}, u32[]{:S(2)}) collective-permute-start(bf16[2,32,512]{2,1,0:T(8,128)(2,1)S(1)} %get-tuple-element.20), channel_id=1, source_target_pairs={{0,2},{1,3},{2,0},{3,1},{4,6},{5,7},{6,4},{7,5},{8,10},{9,11},{10,... | collective-permute-start | bytes 196616 | tf_op jit(solution)/shard_map/ppermute | solution.py:345
  138.8 23.7 %collective-permute-start.2 = (bf16[2,32,512]{2,1,0:T(8,128)(2,1)S(1)}, bf16[2,32,512]{2,1,0:T(8,128)(2,1)S(1)}, u32[]{:S(2)}, u32[]{:S(2)}) collective-permute-start(bf16[2,32,512]{2,1,0:T(8,128)(2,1)S(1)} %get-tuple-element.21), channel_id=1, source_target_pairs={{0,3},{1,0},{2,1},{3,2},{4,7},{5,4},{6,5},{7,6},{8,11},{9,8},{10,9... | collective-permute-start | bytes 196616 | tf_op jit(solution)/shard_map/ppermute | solution.py:345
  157.5 5.2 %collective-permute-start.3 = (bf16[2,32,512]{2,1,0:T(8,128)(2,1)S(1)}, bf16[2,32,512]{2,1,0:T(8,128)(2,1)S(1)}, u32[]{:S(2)}, u32[]{:S(2)}) collective-permute-start(bf16[2,32,512]{2,1,0:T(8,128)(2,1)S(1)} %get-tuple-element.24), channel_id=1, source_target_pairs={{0,1},{1,2},{2,3},{3,0},{4,5},{5,6},{6,7},{7,4},{8,9},{9,10},{10,1... | collective-permute-start | bytes 196616 | tf_op jit(solution)/shard_map/ppermute | solution.py:345
  158.8 6.3 %collective-permute-start.4 = (bf16[2,32,512]{2,1,0:T(8,128)(2,1)S(1)}, bf16[2,32,512]{2,1,0:T(8,128)(2,1)S(1)}, u32[]{:S(2)}, u32[]{:S(2)}) collective-permute-start(bf16[2,32,512]{2,1,0:T(8,128)(2,1)S(1)} %get-tuple-element.25), channel_id=1, source_target_pairs={{0,2},{1,3},{2,0},{3,1},{4,6},{5,7},{6,4},{7,5},{8,10},{9,11},{10,... | collective-permute-start | bytes 196616 | tf_op jit(solution)/shard_map/ppermute | solution.py:345
  161.5 3.7 %collective-permute-start.5 = (bf16[2,32,512]{2,1,0:T(8,128)(2,1)S(1)}, bf16[2,32,512]{2,1,0:T(8,128)(2,1)S(1)}, u32[]{:S(2)}, u32[]{:S(2)}) collective-permute-start(bf16[2,32,512]{2,1,0:T(8,128)(2,1)S(1)} %get-tuple-element.26), channel_id=1, source_target_pairs={{0,3},{1,0},{2,1},{3,2},{4,7},{5,4},{6,5},{7,6},{8,11},{9,8},{10,9... | collective-permute-start | bytes 196616 | tf_op jit(solution)/shard_map/ppermute | solution.py:345

commit v5 on v4

--- a/solution.py
+++ b/solution.py
@@ -261,7 +261,7 @@
             out_shape=jax.ShapeDtypeStruct((sources, count) + group, bf16),
             in_specs=[whole()] * 2,
             out_specs=whole(),
-            compiler_params=small,
+            compiler_params=params if first else small,
             name="dispatch",
         )(flat_queries, turned)
 

time: 167 us -> 167 us (level)
    unnamed x21 -> x19, local copies, waits for them, and re-layouts: 3.4 us -> 3.41 us
  transfers between devices with their start and end apart: 10 -> 10, of which waited for: 6 -> 6; matrix products, arithmetic and copies ran while one was open for 6% -> 6% of each run, Pallas kernels for 23% -> 24%
where the time goes in v5:
time: 167 us; the launch traced here: 166 us
  waiting for transfers between devices  67.1 us (40%)
  Pallas kernels  43.4 us (26%)
  starting transfers between devices  41.9 us (25%)
  local copies, waits for them, and re-layouts  13.5 us (8%)
    all_to_all x2, waiting for transfers between devices, local(): received = [lax.all_to_all(item, 'ctx', 0, 0, tiled=True) for item in sent]  32.4 us
    all_to_all x2, waiting for transfers between devices, local(): back = [lax.all_to_all(item, 'ctx', 0, 0, tiled=True) for item in parts]  32.1 us
    pallas_call x2, Pallas kernels, far(): pl.pallas_call(lambda *refs: far_kernel(scale, count, *refs), grid=(count...  27.2 us
    all_to_all x2, starting transfers between devices, local(): received = [lax.all_to_all(item, 'ctx', 0, 0, tiled=True) for item in sent]  19.2 us
    all_to_all x2, starting transfers between devices, local(): back = [lax.all_to_all(item, 'ctx', 0, 0, tiled=True) for item in parts]  12.6 us
    ppermute x6, starting transfers between devices, local(): made[step] = lax.ppermute(made[step], 'head', pairs)  10.1 us
    pallas_call x2, Pallas kernels, dispatch(): pl.pallas_call(lambda *refs: dispatch_kernel(first, sources, capacity, he...  5.93 us
    pallas_call x1, Pallas kernels, local(): pl.pallas_call(lambda *refs: near_kernel(sources, capacity, heads, width,...  5.7 us
  transfers between devices with their start and end apart: 10, of which 6 were waited for; matrix products, arithmetic and copies ran while one was open for 6% of the time, Pallas kernels for 24%

profile of v5, /device:TPU:1, one launch (start us, length us, event | category | flops | bytes accessed | tf_op | source)
XLA Modules:
  0.0 166.1 jit_solution(1557373075085067730)
XLA Ops:
  0.0 1.1 copy.17
  1.1 0.0 copy-start.1
  1.2 0.0 copy-start.2
  1.2 0.7 copy-done.2
  1.9 2.5 %dispatch.2 = bf16[64,2,32,128]{3,2,1,0:T(8,128)(2,1)} custom-call(bf16[128,2048]{1,0:T(8,128)(2,1)S(1)} %bitcast.20, s32[3,4,128]{2,1,0:T(4,128)S(1)} %bitcast.25), custom_call_target="tpu_custom_call" | custom-call | tf_op jit(solution)/shard_map/dispatch/pallas_call | solution.py:259
  4.3 0.0 copy-done.1
  4.3 13.0 %all-to-all-start = ((bf16[64,2,32,128]{3,2,1,0:T(8,128)(2,1)}), bf16[64,2,32,128]{3,2,1,0:T(8,128)(2,1)S(1)}, u32[]{:S(2)}, u32[]{:S(2)}) async-start(bf16[64,2,32,128]{3,2,1,0:T(8,128)(2,1)} %dispatch.2), calls=%async_computation | async-start | bytes 2097152 | tf_op jit(solution)/shard_map/all_to_all | solution.py:302
  17.3 3.5 %dispatch.3 = bf16[64,2,32,128]{3,2,1,0:T(8,128)(2,1)} custom-call(bf16[128,2048]{1,0:T(8,128)(2,1)} %bitcast.21, s32[3,4,128]{2,1,0:T(4,128)} %bitcast.23), custom_call_target="tpu_custom_call" | custom-call | tf_op jit(solution)/shard_map/dispatch/pallas_call | solution.py:259
  20.8 25.1 %all-to-all-done.refs_0_ = bf16[64,2,32,128]{3,2,1,0:T(8,128)(2,1)S(1)} async-done(((bf16[64,2,32,128]{3,2,1,0:T(8,128)(2,1)}), bf16[64,2,32,128]{3,2,1,0:T(8,128)(2,1)S(1)}, u32[]{:S(2)}, u32[]{:S(2)}) %all-to-all-start) | async-done | bytes 1048608 | tf_op jit(solution)/shard_map/all_to_all | solution.py:302
  45.9 1.0 copy-done.5
  46.9 6.2 %all-to-all-start.2 = ((bf16[64,2,32,128]{3,2,1,0:T(8,128)(2,1)}), bf16[64,2,32,128]{3,2,1,0:T(8,128)(2,1)S(1)}, u32[]{:S(2)}, u32[]{:S(2)}) async-start(bf16[64,2,32,128]{3,2,1,0:T(8,128)(2,1)} %dispatch.3), calls=%async_computation.2 | async-start | bytes 2097152 | tf_op jit(solution)/shard_map/all_to_all | solution.py:302
  53.1 0.0 copy-done.3
  53.1 4.2 %copy_bitcast_fusion = (bf16[2048,512]{1,0:T(8,128)(2,1)}, bf16[2048,512]{1,0:T(8,128)(2,1)}) fusion(bf16[256,8,4,128]{3,2,1,0:T(4,128)(2,1)S(1)} %bitcast.28, bf16[256,8,4,128]{3,2,1,0:T(4,128)(2,1)} %bitcast.29), kind=kLoop, calls=%fused_computation | loop fusion | bytes 8388608 | tf_op jit(solution)/shard_map/reshape | solution.py:271
  57.3 13.6 %far.2 = bf16[64,72,128]{2,1,0:T(8,128)(2,1)} custom-call(bf16[64,2,32,128]{3,2,1,0:T(8,128)(2,1)} %copy-done.5, bf16[2048,512]{1,0:T(8,128)(2,1)} %get-tuple-element.30.refs_1_, bf16[2048,512]{1,0:T(8,128)(2,1)} %get-tuple-element.29.refs_2_), custom_call_target="tpu_custom_call" | custom-call | flops 6442450944 | bytes 2097152 | tf_op jit(solution)/shard_map/far/pallas_call | solution.py:279
  70.9 1.5 copy.13
  72.5 1.9 %copy.14 = bf16[64,17,4,128]{3,2,1,0:T(4,128)(2,1)} copy(bf16[64,17,4,128]{3,0,2,1:T(8,128)(2,1)S(1)} %bitcast.26) | data formatting | bytes 2228224 | tf_op jit(solution)/shard_map/reshape | solution.py:305
  74.3 7.3 %all-to-all-done.2.refs_0_ = bf16[64,2,32,128]{3,2,1,0:T(8,128)(2,1)S(1)} async-done(((bf16[64,2,32,128]{3,2,1,0:T(8,128)(2,1)}), bf16[64,2,32,128]{3,2,1,0:T(8,128)(2,1)S(1)}, u32[]{:S(2)}, u32[]{:S(2)}) %all-to-all-start.2) | async-done | bytes 1048608 | tf_op jit(solution)/shard_map/all_to_all | solution.py:302
  81.7 6.4 %all-to-all-start.1 = ((bf16[64,17,4,128]{3,2,1,0:T(4,128)(2,1)}), bf16[64,17,4,128]{3,2,1,0:T(4,128)(2,1)S(1)}, u32[]{:S(2)}, u32[]{:S(2)}) async-start(bf16[64,17,4,128]{3,2,1,0:T(4,128)(2,1)} %copy.14), calls=%async_computation.1 | async-start | bytes 2228224 | tf_op jit(solution)/shard_map/all_to_all | solution.py:306
  88.0 0.0 copy-done.4
  88.0 13.6 %far.3 = bf16[64,72,128]{2,1,0:T(8,128)(2,1)} custom-call(bf16[64,2,32,128]{3,2,1,0:T(8,128)(2,1)} %copy-done.4, bf16[2048,512]{1,0:T(8,128)(2,1)} %get-tuple-element.30.refs_1_, bf16[2048,512]{1,0:T(8,128)(2,1)} %get-tuple-element.29.refs_2_), custom_call_target="tpu_custom_call" | custom-call | flops 6442450944 | bytes 2097152 | tf_op jit(solution)/shard_map/far/pallas_call | solution.py:279
  101.7 16.3 %all-to-all-done.1 = bf16[64,17,4,128]{3,2,1,0:T(4,128)(2,1)S(1)} async-done(((bf16[64,17,4,128]{3,2,1,0:T(4,128)(2,1)}), bf16[64,17,4,128]{3,2,1,0:T(4,128)(2,1)S(1)}, u32[]{:S(2)}, u32[]{:S(2)}) %all-to-all-start.1) | async-done | bytes 1114144 | tf_op jit(solution)/shard_map/all_to_all | solution.py:306
  118.0 6.2 %all-to-all-start.3 = ((bf16[64,72,128]{2,1,0:T(8,128)(2,1)}), bf16[64,72,128]{2,1,0:T(8,128)(2,1)S(1)}, u32[]{:S(2)}, u32[]{:S(2)}) async-start(bf16[64,72,128]{2,1,0:T(8,128)(2,1)} %far.3), calls=%async_computation.3 | async-start | bytes 2359296 | tf_op jit(solution)/shard_map/all_to_all | solution.py:306
  124.2 0.0 copy-done.8
  124.2 0.7 copy.12.refs_5_
  125.0 0.0 copy-done.6
  125.0 0.0 copy-done.7
  125.0 0.7 copy_bitcast_fusion.2
  125.7 5.7 %near.1.refs_1_ = f32[128,2304]{1,0:T(8,128)} custom-call(bf16[128,2048]{1,0:T(8,128)(2,1)} %bitcast.22, bf16[128,512]{1,0:T(8,128)(2,1)} %get-tuple-element.28.refs_1_, bf16[128,512]{1,0:T(8,128)(2,1)} %get-tuple-element.27.refs_2_, s32[3,4,128]{2,1,0:T(4,128)} %bitcast.24, s32[1,128]{1,0:T(1,128)} %refs_4_.1, s32[128,1]{1,0:T(8,128)} %copy.12.refs_5_), custom_call_target="tpu_custom_call" | custom-call | flops 134217728 | bytes 4194304 | tf_op jit(solution)/shard_map/near/pallas_call | solution.py:309
  131.4 0.3 copy.15
  131.7 0.0 copy-start
  131.7 0.7 copy.16.refs_2_
  132.4 0.5 copy-done
  132.9 1.8 %merge.2 = (bf16[2,32,512]{2,1,0:T(8,128)(2,1)S(1)}, bf16[2,32,512]{2,1,0:T(8,128)(2,1)S(1)}, bf16[2,32,512]{2,1,0:T(8,128)(2,1)S(1)}, bf16[2,32,512]{2,1,0:T(8,128)(2,1)S(1)}) custom-call(s32[1]{0:T(128)} %bitcast.refs_0_, f32[128,2304]{1,0:T(8,128)S(1)} %copy-done, bf16[64,68,128]{2,1,0:T(8,128)(2,1)S(1)} %copy.16.refs_2_), custom_call_target="tpu_custom_call" | custom-call | tf_op jit(solution)/shard_map/merge/pallas_call | solution.py:333
  134.7 1.4 collective-permute-start
  136.1 2.6 %collective-permute-start.1 = (bf16[2,32,512]{2,1,0:T(8,128)(2,1)S(1)}, bf16[2,32,512]{2,1,0:T(8,128)(2,1)S(1)}, u32[]{:S(2)}, u32[]{:S(2)}) collective-permute-start(bf16[2,32,512]{2,1,0:T(8,128)(2,1)S(1)} %get-tuple-element.20), channel_id=1, source_target_pairs={{0,2},{1,3},{2,0},{3,1},{4,6},{5,7},{6,4},{7,5},{8,10},{9,11},{10,... | collective-permute-start | bytes 196616 | tf_op jit(solution)/shard_map/ppermute | solution.py:345
  138.7 1.1 collective-permute-start.2
  139.8 15.8 %all-to-all-done.3.refs_2_ = bf16[64,72,128]{2,1,0:T(8,128)(2,1)S(1)} async-done(((bf16[64,72,128]{2,1,0:T(8,128)(2,1)}), bf16[64,72,128]{2,1,0:T(8,128)(2,1)S(1)}, u32[]{:S(2)}, u32[]{:S(2)}) %all-to-all-start.3) | async-done | bytes 1179680 | tf_op jit(solution)/shard_map/all_to_all | solution.py:306
  155.6 1.8 %merge.3 = (bf16[2,32,512]{2,1,0:T(8,128)(2,1)S(1)}, bf16[2,32,512]{2,1,0:T(8,128)(2,1)S(1)}, bf16[2,32,512]{2,1,0:T(8,128)(2,1)S(1)}, bf16[2,32,512]{2,1,0:T(8,128)(2,1)S(1)}) custom-call(s32[1]{0:T(128)} %bitcast.refs_0_, f32[128,2304]{1,0:T(8,128)S(1)} %copy-done, bf16[64,72,128]{2,1,0:T(8,128)(2,1)S(1)} %all-to-all-done.3.refs_2_), custom_call_target="tpu_custom_call" | custom-call | tf_op jit(solution)/shard_map/merge/pallas_call | solution.py:333
  157.3 1.4 collective-permute-start.3
  158.7 2.6 %collective-permute-start.4 = (bf16[2,32,512]{2,1,0:T(8,128)(2,1)S(1)}, bf16[2,32,512]{2,1,0:T(8,128)(2,1)S(1)}, u32[]{:S(2)}, u32[]{:S(2)}) collective-permute-start(bf16[2,32,512]{2,1,0:T(8,128)(2,1)S(1)} %get-tuple-element.25), channel_id=1, source_target_pairs={{0,2},{1,3},{2,0},{3,1},{4,6},{5,7},{6,4},{7,5},{8,10},{9,11},{10,... | collective-permute-start | bytes 196616 | tf_op jit(solution)/shard_map/ppermute | solution.py:345
  161.3 0.0 collective-permute-done.refs_2_
  161.3 1.1 collective-permute-start.5
  162.4 0.0 collective-permute-done.1.refs_3_
  162.4 0.0 collective-permute-done.2.refs_4_
  162.4 0.1 collective-permute-done.3.refs_6_
  162.5 2.5 %collective-permute-done.4.refs_7_ = bf16[2,32,512]{2,1,0:T(8,128)(2,1)S(1)} collective-permute-done((bf16[2,32,512]{2,1,0:T(8,128)(2,1)S(1)}, bf16[2,32,512]{2,1,0:T(8,128)(2,1)S(1)}, u32[]{:S(2)}, u32[]{:S(2)}) %collective-permute-start.4) | collective-permute-done | bytes 65568 | tf_op jit(solution)/shard_map/ppermute | solution.py:345
  165.0 0.0 collective-permute-done.5.refs_8_
  165.0 1.1 assemble.1
  (6 shorter events, 0.0 us)
Async XLA Ops:
  1.1 3.2 %copy-start.1 = (bf16[16,8,4,512]{3,1,2,0:T(8,128)(2,1)}, bf16[16,8,4,512]{3,1,2,0:T(8,128)(2,1)S(1)}, u32[]{:S(2)}) copy-start(bf16[16,8,4,512]{3,1,2,0:T(8,128)(2,1)S(1)} %copy.17) | copy-start | bytes 1572868
  1.2 0.7 copy-start.2
  4.3 41.6 %all-to-all-start = ((bf16[64,2,32,128]{3,2,1,0:T(8,128)(2,1)}), bf16[64,2,32,128]{3,2,1,0:T(8,128)(2,1)S(1)}, u32[]{:S(2)}, u32[]{:S(2)}) async-start(bf16[64,2,32,128]{3,2,1,0:T(8,128)(2,1)} %dispatch.2), calls=%async_computation | async-start | bytes 2097152 | tf_op jit(solution)/shard_map/all_to_all | solution.py:302
  20.8 32.3 %copy-start.3 = (bf16[2048,4,128]{2,1,0:T(4,128)(2,1)S(1)}, bf16[2048,4,128]{2,1,0:T(4,128)(2,1)}, u32[]{:S(2)}) copy-start(bf16[2048,4,128]{2,1,0:T(4,128)(2,1)} %param.9) | copy-start | bytes 6291460
  45.9 1.0 copy-start.5
  46.9 34.8 %all-to-all-start.2 = ((bf16[64,2,32,128]{3,2,1,0:T(8,128)(2,1)}), bf16[64,2,32,128]{3,2,1,0:T(8,128)(2,1)S(1)}, u32[]{:S(2)}, u32[]{:S(2)}) async-start(bf16[64,2,32,128]{3,2,1,0:T(8,128)(2,1)} %dispatch.3), calls=%async_computation.2 | async-start | bytes 2097152 | tf_op jit(solution)/shard_map/all_to_all | solution.py:302
  81.7 6.4 %copy-start.4 = (bf16[64,2,32,128]{3,2,1,0:T(8,128)(2,1)}, bf16[64,2,32,128]{3,2,1,0:T(8,128)(2,1)S(1)}, u32[]{:S(2)}) copy-start(bf16[64,2,32,128]{3,2,1,0:T(8,128)(2,1)S(1)} %all-to-all-done.2.refs_0_) | copy-start | bytes 3145732
  81.7 36.3 %all-to-all-start.1 = ((bf16[64,17,4,128]{3,2,1,0:T(4,128)(2,1)}), bf16[64,17,4,128]{3,2,1,0:T(4,128)(2,1)S(1)}, u32[]{:S(2)}, u32[]{:S(2)}) async-start(bf16[64,17,4,128]{3,2,1,0:T(4,128)(2,1)} %copy.14), calls=%async_computation.1 | async-start | bytes 2228224 | tf_op jit(solution)/shard_map/all_to_all | solution.py:306
  101.7 22.6 %copy-start.8 = (s32[1,128]{1,0:T(1,128)S(1)}, s32[1,128]{1,0:T(1,128)}, u32[]{:S(2)}) copy-start(s32[1,128]{1,0:T(1,128)} %refs_4_.1) | copy-start | bytes 1540
  101.7 23.3 %copy-start.6 = (bf16[128,4,128]{2,1,0:T(4,128)(2,1)S(1)}, bf16[128,4,128]{2,1,0:T(4,128)(2,1)}, u32[]{:S(2)}) copy-start(bf16[128,4,128]{2,1,0:T(4,128)(2,1)} %param.11) | copy-start | bytes 393220
  101.7 23.3 %copy-start.7 = (bf16[128,4,128]{2,1,0:T(4,128)(2,1)S(1)}, bf16[128,4,128]{2,1,0:T(4,128)(2,1)}, u32[]{:S(2)}) copy-start(bf16[128,4,128]{2,1,0:T(4,128)(2,1)} %param.10) | copy-start | bytes 393220
  118.0 37.6 %all-to-all-start.3 = ((bf16[64,72,128]{2,1,0:T(8,128)(2,1)}), bf16[64,72,128]{2,1,0:T(8,128)(2,1)S(1)}, u32[]{:S(2)}, u32[]{:S(2)}) async-start(bf16[64,72,128]{2,1,0:T(8,128)(2,1)} %far.3), calls=%async_computation.3 | async-start | bytes 2359296 | tf_op jit(solution)/shard_map/all_to_all | solution.py:306
  131.7 1.3 copy-start
  134.7 26.6 %collective-permute-start = (bf16[2,32,512]{2,1,0:T(8,128)(2,1)S(1)}, bf16[2,32,512]{2,1,0:T(8,128)(2,1)S(1)}, u32[]{:S(2)}, u32[]{:S(2)}) collective-permute-start(bf16[2,32,512]{2,1,0:T(8,128)(2,1)S(1)} %get-tuple-element.19), channel_id=1, source_target_pairs={{0,1},{1,2},{2,3},{3,0},{4,5},{5,6},{6,7},{7,4},{8,9},{9,10},{10,1... | collective-permute-start | bytes 196616 | tf_op jit(solution)/shard_map/ppermute | solution.py:345
  136.1 26.3 %collective-permute-start.1 = (bf16[2,32,512]{2,1,0:T(8,128)(2,1)S(1)}, bf16[2,32,512]{2,1,0:T(8,128)(2,1)S(1)}, u32[]{:S(2)}, u32[]{:S(2)}) collective-permute-start(bf16[2,32,512]{2,1,0:T(8,128)(2,1)S(1)} %get-tuple-element.20), channel_id=1, source_target_pairs={{0,2},{1,3},{2,0},{3,1},{4,6},{5,7},{6,4},{7,5},{8,10},{9,11},{10,... | collective-permute-start | bytes 196616 | tf_op jit(solution)/shard_map/ppermute | solution.py:345
  138.7 23.7 %collective-permute-start.2 = (bf16[2,32,512]{2,1,0:T(8,128)(2,1)S(1)}, bf16[2,32,512]{2,1,0:T(8,128)(2,1)S(1)}, u32[]{:S(2)}, u32[]{:S(2)}) collective-permute-start(bf16[2,32,512]{2,1,0:T(8,128)(2,1)S(1)} %get-tuple-element.21), channel_id=1, source_target_pairs={{0,3},{1,0},{2,1},{3,2},{4,7},{5,4},{6,5},{7,6},{8,11},{9,8},{10,9... | collective-permute-start | bytes 196616 | tf_op jit(solution)/shard_map/ppermute | solution.py:345
  157.3 5.1 %collective-permute-start.3 = (bf16[2,32,512]{2,1,0:T(8,128)(2,1)S(1)}, bf16[2,32,512]{2,1,0:T(8,128)(2,1)S(1)}, u32[]{:S(2)}, u32[]{:S(2)}) collective-permute-start(bf16[2,32,512]{2,1,0:T(8,128)(2,1)S(1)} %get-tuple-element.24), channel_id=1, source_target_pairs={{0,1},{1,2},{2,3},{3,0},{4,5},{5,6},{6,7},{7,4},{8,9},{9,10},{10,1... | collective-permute-start | bytes 196616 | tf_op jit(solution)/shard_map/ppermute | solution.py:345
  158.7 6.3 %collective-permute-start.4 = (bf16[2,32,512]{2,1,0:T(8,128)(2,1)S(1)}, bf16[2,32,512]{2,1,0:T(8,128)(2,1)S(1)}, u32[]{:S(2)}, u32[]{:S(2)}) collective-permute-start(bf16[2,32,512]{2,1,0:T(8,128)(2,1)S(1)} %get-tuple-element.25), channel_id=1, source_target_pairs={{0,2},{1,3},{2,0},{3,1},{4,6},{5,7},{6,4},{7,5},{8,10},{9,11},{10,... | collective-permute-start | bytes 196616 | tf_op jit(solution)/shard_map/ppermute | solution.py:345
  161.3 3.7 %collective-permute-start.5 = (bf16[2,32,512]{2,1,0:T(8,128)(2,1)S(1)}, bf16[2,32,512]{2,1,0:T(8,128)(2,1)S(1)}, u32[]{:S(2)}, u32[]{:S(2)}) collective-permute-start(bf16[2,32,512]{2,1,0:T(8,128)(2,1)S(1)} %get-tuple-element.26), channel_id=1, source_target_pairs={{0,3},{1,0},{2,1},{3,2},{4,7},{5,4},{6,5},{7,6},{8,11},{9,8},{10,9... | collective-permute-start | bytes 196616 | tf_op jit(solution)/shard_map/ppermute | solution.py:345
